TPU v7x, 32 devices: a whole 2x2x4 slice. The times are simulated.
32 devices in a mesh: fsdp: 4 (over y, x), expert: 2 (over core), tensor: 4 (over z).
Axes of the slice: x: 2, y: 2, z: 4, core: 2. Of those that a mesh axis runs over, the one named last changes fastest.
Arguments:
- tokens: bfloat16 [6304, 768], P(('fsdp', 'expert')), may hold values from -6 to 6
- routes: int32 [6304, 2], P(('fsdp', 'expert')), may hold values from 0 to 7, all different within a row; in each aligned block of 788 rows (0 to 787, 788 to 1575, ...) at most 296 rows name the same one
- cotangent: bfloat16 [6304, 768], P(('fsdp', 'expert')), may hold values from -6 to 6
- ln_gain: bfloat16 [2, 2, 768], P(None, None, 'fsdp'), may hold values from 0.5 to 1.5
- ln_bias: bfloat16 [2, 2, 768], P(None, None, 'fsdp'), may hold values from -3 to 3
- w_qkv: bfloat16 [2, 768, 3, 768], P(None, 'fsdp', None, 'tensor'), may hold values from -0.21875 to 0.21875
- w_out: bfloat16 [2, 768, 768], P(None, 'tensor', 'fsdp'), may hold values from -1.5 to 1.5
- w_router: bfloat16 [2, 768, 8], P(None, 'fsdp'), may hold values from -0.15625 to 0.15625
- w_in: bfloat16 [2, 8, 768, 3072], P(None, ('fsdp', 'expert'), None, 'tensor'), may hold values from -0.21875 to 0.21875
- w_back: bfloat16 [2, 8, 3072, 768], P(None, ('fsdp', 'expert'), 'tensor'), may hold values from -1 to 1
Outputs:
- output: bfloat16 [6304, 768], P(('fsdp', 'expert'))
- grad_tokens: float32 [6304, 768], P(('fsdp', 'expert'))
- grad_ln_gain: float32 [2, 2, 768], P(None, None, 'fsdp')
- grad_ln_bias: float32 [2, 2, 768], P(None, None, 'fsdp')
- grad_qkv: float32 [2, 768, 3, 768], P(None, 'fsdp', None, 'tensor')
- grad_out: float32 [2, 768, 768], P(None, 'tensor', 'fsdp')
- grad_router: float32 [2, 768, 8], P(None, 'fsdp')
- grad_in: float32 [2, 8, 768, 3072], P(None, ('fsdp', 'expert'), None, 'tensor')
- grad_back: float32 [2, 8, 3072, 768], P(None, ('fsdp', 'expert'), 'tensor')
Inputs may be any that keep to these rules, and one draw needn't show every extreme that they name: `routes`: each row names 2 different experts. In the rows of one index of fsdp and expert (aligned blocks of 788 rows) no expert is named more than 296 times, a bound that some block reaches.
All inputs are finite; a program needn't handle non-finite values.
Results may differ from a plain program's by a relative error of at most 0.02.
Values may be sent and summed in bfloat16 or wider, within the bound.
A program may use at most 192 MiB of HBM per device.

v0:
```python
import jax
import jax.numpy as jnp
from jax import lax
from jax.sharding import PartitionSpec as P

HEAD_DIM = 64
SEQ = 197


epsilon = 1e-06


def for_sending(shard):

    def short(part):
        return part.astype(jnp.bfloat16) if part.dtype == jnp.float32 else part

    return jax.tree.map(short, shard)


def layer_norm(values, gain_row, bias_row):
    center = values - jnp.mean(values, axis=-1, keepdims=True)
    inverse = lax.rsqrt(jnp.mean(center * center, axis=-1, keepdims=True) + epsilon)
    scaled = center * inverse
    return (scaled * gain_row + bias_row, scaled, inverse)


def norm_back(grad_out, scaled, inverse, gain_row):
    grad_scaled = grad_out * gain_row
    grad_values = inverse * (
        grad_scaled
        - jnp.mean(grad_scaled, axis=-1, keepdims=True)
        - scaled * jnp.mean(grad_scaled * scaled, axis=-1, keepdims=True)
    )
    return (grad_values, jnp.sum(grad_out * scaled, axis=0), jnp.sum(grad_out, axis=0))


def slot_positions(routes_dev, expert_count, capacity):
    onehot = (
        routes_dev[:, :, None] == jnp.arange(expert_count, dtype=jnp.int32)[None, None, :]
    ).astype(jnp.int32)
    per_token = jnp.sum(onehot, axis=1)
    earlier = jnp.cumsum(per_token, axis=0) - per_token
    slots = jnp.sum(earlier[:, None, :] * onehot, axis=-1)
    return routes_dev * capacity + slots


def move_rows(buffer):
    return lax.all_to_all(buffer, ("fsdp", "expert"), split_axis=0, concat_axis=0, tiled=True)


def contract_first(left, right):
    return lax.dot_general(
        left, right, (((0,), (0,)), ((), ())), preferred_element_type=jnp.float32
    )


def contract_last(left, right):
    return lax.dot_general(
        left, right, (((1,), (1,)), ((), ())), preferred_element_type=jnp.float32
    )


def on_device(tokens, routes, cotangent, ln_gain, ln_bias, w_qkv, w_out, w_router, w_in, w_back):
    tok_rows = tokens.shape[0]
    feat_width = tokens.shape[1]
    top_count = routes.shape[1]
    experts = lax.axis_size(("fsdp", "expert"))
    tensor_width = lax.axis_size("tensor")
    capacity = (3 * tok_rows * top_count // (2 * experts) + 7) // 8 * 8
    slot_rows = experts * capacity
    images = tok_rows // SEQ
    head_cols = w_qkv.shape[3]
    local_heads = head_cols // HEAD_DIM
    scale_factor = HEAD_DIM ** (-0.5)
    layer_count = w_qkv.shape[0]
    positions = slot_positions(routes, experts, capacity)
    flat_positions = positions.reshape(-1)
    route_table = (
        routes[:, :, None] == jnp.arange(experts, dtype=jnp.int32)[None, None, :]
    ).astype(jnp.float32)
    residual = tokens.astype(jnp.float32)
    kept_layer = []
    for layer_idx in range(layer_count):
        weight_qkv, weight_out, weight_router, gain_pair, bias_pair = (
            lax.all_gather(w_qkv[layer_idx], "fsdp", axis=0, tiled=True),
            lax.all_gather(w_out[layer_idx], "fsdp", axis=1, tiled=True),
            lax.all_gather(w_router[layer_idx], "fsdp", axis=0, tiled=True),
            lax.all_gather(ln_gain[layer_idx], "fsdp", axis=1, tiled=True),
            lax.all_gather(ln_bias[layer_idx], "fsdp", axis=1, tiled=True),
        )
        gain_pair = gain_pair.astype(jnp.float32)
        bias_pair = bias_pair.astype(jnp.float32)
        normed, scaled_first, inverse_first = layer_norm(residual, gain_pair[0], bias_pair[0])
        normed = normed.astype(jnp.bfloat16)
        mixed_qkv = jnp.einsum(
            "td,dcj->tcj", normed, weight_qkv, preferred_element_type=jnp.float32
        ).astype(jnp.bfloat16)
        heads_view = mixed_qkv.reshape(images, SEQ, 3, local_heads, HEAD_DIM)
        queries = heads_view[:, :, 0]
        keys_all = heads_view[:, :, 1]
        values_all = heads_view[:, :, 2]
        scores = (
            jnp.einsum("ishd,ithd->ihst", queries, keys_all, preferred_element_type=jnp.float32)
            * scale_factor
        )
        row_peak = jnp.max(scores, axis=-1, keepdims=True)
        log_total = row_peak + jnp.log(jnp.sum(jnp.exp(scores - row_peak), axis=-1, keepdims=True))
        probs_low = jnp.exp(scores - log_total).astype(jnp.bfloat16)
        attended = jnp.einsum(
            "ihst,ithd->ishd", probs_low, values_all, preferred_element_type=jnp.float32
        )
        attended = attended.reshape(tok_rows, head_cols).astype(jnp.bfloat16)
        branch = lax.psum(
            jnp.dot(attended, weight_out, preferred_element_type=jnp.float32), "tensor"
        )
        middle = residual + branch
        routed, scaled_second, inverse_second = layer_norm(middle, gain_pair[1], bias_pair[1])
        routed = routed.astype(jnp.bfloat16)
        logits = jnp.dot(routed, weight_router, preferred_element_type=jnp.float32)
        gate_probs = jax.nn.softmax(logits, axis=-1)
        combine = jnp.sum(gate_probs[:, None, :] * route_table, axis=-1)
        buffer = (
            jnp.zeros((slot_rows, feat_width), jnp.bfloat16)
            .at[flat_positions]
            .set(jnp.repeat(routed, top_count, axis=0))
        )
        arrived = move_rows(buffer.reshape(experts, capacity, feat_width)).reshape(
            slot_rows, feat_width
        )
        pre_act = jnp.dot(arrived, w_in[layer_idx, 0], preferred_element_type=jnp.float32)
        hidden = jax.nn.gelu(pre_act, approximate=False).astype(jnp.bfloat16)
        partial_out = jnp.dot(hidden, w_back[layer_idx, 0], preferred_element_type=jnp.float32)
        col_share = lax.psum_scatter(partial_out, "tensor", scatter_dimension=1, tiled=True).astype(
            jnp.bfloat16
        )
        share_cols = col_share.shape[1]
        returned = move_rows(col_share.reshape(experts, capacity, share_cols))
        picked = returned.reshape(slot_rows, share_cols)[positions]
        mixture = lax.all_gather(
            jnp.sum(combine[:, :, None] * picked.astype(jnp.float32), axis=1).astype(jnp.bfloat16),
            "tensor",
            axis=1,
            tiled=True,
        ).astype(jnp.float32)
        kept_layer.append(
            (
                weight_qkv,
                weight_out,
                weight_router,
                gain_pair,
                normed,
                scaled_first,
                inverse_first,
                queries,
                keys_all,
                values_all,
                log_total,
                attended,
                routed,
                scaled_second,
                inverse_second,
                gate_probs,
                combine,
                arrived,
                pre_act,
                hidden,
                picked,
            )
        )
        residual = middle + mixture
    output = residual.astype(jnp.bfloat16)
    grad_res = cotangent.astype(jnp.float32)
    gain_grads = [None] * layer_count
    bias_grads = [None] * layer_count
    qkv_grads = [None] * layer_count
    out_grads = [None] * layer_count
    router_grads = [None] * layer_count
    in_grads = [None] * layer_count
    back_grads = [None] * layer_count
    for layer_idx in reversed(range(layer_count)):
        (
            weight_qkv,
            weight_out,
            weight_router,
            gain_pair,
            normed,
            scaled_first,
            inverse_first,
            queries,
            keys_all,
            values_all,
            log_total,
            attended,
            routed,
            scaled_second,
            inverse_second,
            gate_probs,
            combine,
            arrived,
            pre_act,
            hidden,
            picked,
        ) = kept_layer[layer_idx]
        share_cols = picked.shape[2]
        own_columns = lax.dynamic_slice_in_dim(
            grad_res, lax.axis_index("tensor") * share_cols, share_cols, 1
        )
        dot_partial = jnp.sum(own_columns[:, None, :] * picked.astype(jnp.float32), axis=-1)
        slot_grads = (
            (combine[:, :, None] * grad_res[:, None, :])
            .astype(jnp.bfloat16)
            .reshape(tok_rows * top_count, feat_width)
        )
        grad_buffer = (
            jnp.zeros((slot_rows, feat_width), jnp.bfloat16).at[flat_positions].set(slot_grads)
        )
        grad_slots = move_rows(grad_buffer.reshape(experts, capacity, feat_width)).reshape(
            slot_rows, feat_width
        )
        weight_back = w_back[layer_idx, 0]
        weight_in = w_in[layer_idx, 0]
        grad_hidden = contract_last(grad_slots, weight_back)
        back_grads[layer_idx] = contract_first(hidden, grad_slots)
        unused_value, gelu_pull = jax.vjp(
            lambda inner_val: jax.nn.gelu(inner_val, approximate=False), pre_act
        )
        grad_pre = gelu_pull(grad_hidden)[0].astype(jnp.bfloat16)
        in_grads[layer_idx] = contract_first(arrived, grad_pre)
        partial_in = contract_last(grad_pre, weight_in)
        grad_share = lax.psum_scatter(
            partial_in.astype(jnp.bfloat16), "tensor", scatter_dimension=1, tiled=True
        )
        share_cols = grad_share.shape[1]
        grad_returned = move_rows(grad_share.reshape(experts, capacity, share_cols)).reshape(
            slot_rows, share_cols
        )
        routed_share = jnp.sum(grad_returned[positions].astype(jnp.float32), axis=1)
        grad_routed, dot_pieces = (
            lax.all_gather(routed_share.astype(jnp.bfloat16), "tensor", axis=1, tiled=True).astype(
                routed_share.dtype
            ),
            lax.all_gather(for_sending(dot_partial), "tensor", axis=1, tiled=True).astype(
                dot_partial.dtype
            ),
        )
        gate_dots = jnp.sum(dot_pieces.reshape(tok_rows, tensor_width, top_count), axis=1)
        grad_gates = jnp.sum(gate_dots[:, :, None] * route_table, axis=1)
        grad_logits = (
            gate_probs * (grad_gates - jnp.sum(gate_probs * grad_gates, axis=-1, keepdims=True))
        ).astype(jnp.bfloat16)
        router_grads[layer_idx] = contract_first(routed, grad_logits)
        grad_routed = grad_routed + contract_last(grad_logits, weight_router)
        grad_norm_two, gain_two, bias_two = norm_back(
            grad_routed, scaled_second, inverse_second, gain_pair[1]
        )
        grad_middle = grad_res + grad_norm_two
        grad_branch = grad_middle.astype(jnp.bfloat16)
        out_grads[layer_idx] = contract_first(attended, grad_branch)
        grad_attended = contract_last(grad_branch, weight_out).astype(jnp.bfloat16)
        grad_attended = grad_attended.reshape(images, SEQ, local_heads, HEAD_DIM)
        scores = (
            jnp.einsum("ishd,ithd->ihst", queries, keys_all, preferred_element_type=jnp.float32)
            * scale_factor
        )
        probs_full = jnp.exp(scores - log_total)
        probs_low = probs_full.astype(jnp.bfloat16)
        grad_values = jnp.einsum(
            "ihst,ishd->ithd", probs_low, grad_attended, preferred_element_type=jnp.float32
        )
        grad_probs = jnp.einsum(
            "ishd,ithd->ihst", grad_attended, values_all, preferred_element_type=jnp.float32
        )
        grad_scores = (
            probs_full * (grad_probs - jnp.sum(probs_full * grad_probs, axis=-1, keepdims=True))
        ).astype(jnp.bfloat16)
        grad_queries = (
            jnp.einsum("ihst,ithd->ishd", grad_scores, keys_all, preferred_element_type=jnp.float32)
            * scale_factor
        )
        grad_keys = (
            jnp.einsum("ihst,ishd->ithd", grad_scores, queries, preferred_element_type=jnp.float32)
            * scale_factor
        )
        grad_mixed = (
            jnp.stack([grad_queries, grad_keys, grad_values], axis=2)
            .reshape(tok_rows, 3, head_cols)
            .astype(jnp.bfloat16)
        )
        qkv_grads[layer_idx] = jnp.einsum(
            "td,tcj->dcj", normed, grad_mixed, preferred_element_type=jnp.float32
        )
        grad_normed = lax.psum(
            jnp.einsum(
                "tcj,dcj->td", grad_mixed, weight_qkv, preferred_element_type=jnp.float32
            ).astype(jnp.bfloat16),
            "tensor",
        ).astype(jnp.float32)
        grad_norm_one, gain_one, bias_one = norm_back(
            grad_normed, scaled_first, inverse_first, gain_pair[0]
        )
        gain_grads[layer_idx] = jnp.stack([gain_one, gain_two], axis=0)
        bias_grads[layer_idx] = jnp.stack([bias_one, bias_two], axis=0)
        grad_res = grad_middle + grad_norm_one
    summed = (
        lax.psum_scatter(
            jnp.stack(gain_grads).astype(jnp.bfloat16),
            ("fsdp", "expert"),
            scatter_dimension=2,
            tiled=True,
        ).astype(jnp.float32),
        lax.psum_scatter(
            jnp.stack(bias_grads).astype(jnp.bfloat16),
            ("fsdp", "expert"),
            scatter_dimension=2,
            tiled=True,
        ).astype(jnp.float32),
        lax.psum_scatter(
            jnp.stack(qkv_grads).astype(jnp.bfloat16),
            ("fsdp", "expert"),
            scatter_dimension=1,
            tiled=True,
        ).astype(jnp.float32),
        lax.psum_scatter(
            jnp.stack(out_grads).astype(jnp.bfloat16),
            ("fsdp", "expert"),
            scatter_dimension=2,
            tiled=True,
        ).astype(jnp.float32),
        lax.psum_scatter(
            jnp.stack(router_grads).astype(jnp.bfloat16),
            ("fsdp", "expert"),
            scatter_dimension=1,
            tiled=True,
        ).astype(jnp.float32),
    )
    spread = (
        lax.all_gather(summed[0].astype(jnp.bfloat16), "expert", axis=2, tiled=True).astype(
            jnp.float32
        ),
        lax.all_gather(summed[1].astype(jnp.bfloat16), "expert", axis=2, tiled=True).astype(
            jnp.float32
        ),
        lax.all_gather(summed[2].astype(jnp.bfloat16), "expert", axis=1, tiled=True).astype(
            jnp.float32
        ),
        lax.all_gather(summed[3].astype(jnp.bfloat16), "expert", axis=2, tiled=True).astype(
            jnp.float32
        ),
        lax.all_gather(summed[4].astype(jnp.bfloat16), "expert", axis=1, tiled=True).astype(
            jnp.float32
        ),
    )
    grad_in_all = jnp.stack(in_grads)[:, None]
    grad_back_all = jnp.stack(back_grads)[:, None]
    return (
        output,
        grad_res,
        spread[0],
        spread[1],
        spread[2],
        spread[3],
        spread[4],
        grad_in_all,
        grad_back_all,
    )


def solution(mesh):
    in_specs = (
        P(("fsdp", "expert"), None),
        P(("fsdp", "expert"), None),
        P(("fsdp", "expert"), None),
        P(None, None, "fsdp"),
        P(None, None, "fsdp"),
        P(None, "fsdp", None, "tensor"),
        P(None, "tensor", "fsdp"),
        P(None, "fsdp", None),
        P(None, ("fsdp", "expert"), None, "tensor"),
        P(None, ("fsdp", "expert"), "tensor", None),
    )
    out_specs = (
        P(("fsdp", "expert"), None),
        P(("fsdp", "expert"), None),
        P(None, None, "fsdp"),
        P(None, None, "fsdp"),
        P(None, "fsdp", None, "tensor"),
        P(None, "tensor", "fsdp"),
        P(None, "fsdp", None),
        P(None, ("fsdp", "expert"), None, "tensor"),
        P(None, ("fsdp", "expert"), "tensor", None),
    )
    return jax.shard_map(
        on_device, mesh=mesh, in_specs=in_specs, out_specs=out_specs, check_vma=False
    )
```

profile of v0, /device:TPU:0, one launch (start us, length us, event | category | flops | bytes accessed | tf_op | source)
XLA Modules:
  0.0 1672.0 jit_solution(5057562431089562231)
XLA Ops:
  55.6 15.4 all-gather.2
  85.8 95.7 %all-reduce.6.cloned.1.call-done = f32[788,768]{1,0:T(8,128)} async-done(((f32[788,768]{1,0:T(8,128)}), f32[788,768]{1,0:T(8,128)}) %all-reduce.6.cloned.1.call-update) | async-done | bytes 2420752 | tf_op jit(solution)/shard_map/psum | solution.py:114
  208.6 47.1 %all_to_all.40 = bf16[8,296,768]{2,1,0:T(8,128)(2,1)S(1)} all-to-all(bf16[8,296,768]{2,1,0:T(8,128)(2,1)} %bitcast.296), channel_id=1, replica_groups=mesh['fsdp'=4,'expert'=2,'tensor'=4] {'fsdp','expert'}, dimensions={0} | all-to-all | bytes 7274496 | tf_op jit(solution)/shard_map/all_to_all | solution.py:49
  255.6 19.2 %multiply_convert_fusion.1 = (bf16[2368,768]{1,0:T(8,128)(2,1)S(1)}, f32[2368,768]{1,0:T(8,128)}, f32[2368,768]{1,0:T(8,128)}) fusion(bf16[2368,768]{1,0:T(8,128)(2,1)S(1)} %bitcast.298, bf16[2,1,768,768]{3,2,1,0:T(8,128)(2,1)S(1)} %copy-done.95), kind=kOutput, calls=%fused_computation.27 | convolution fusion | flops 2911617024 | bytes 23003136 | tf_op jit(solution)/shard_map/dot_general | solution.py:131
  292.7 116.6 %reduce-scatter.20.cloned.1.call-done = f32[2368,192]{0,1:T(8,128)} async-done(((f32[2368,768]{0,1:T(8,128)}), f32[2368,192]{0,1:T(8,128)}) %reduce-scatter.20.cloned.1.call-update) | async-done | bytes 1818640 | tf_op jit(solution)/shard_map/reduce_scatter | solution.py:134
  422.6 14.1 all-to-all-done.1
  490.5 16.7 all-gather.7
  534.1 97.6 %all-reduce.8.cloned.1.call-done = f32[788,768]{1,0:T(8,128)} async-done(((f32[788,768]{1,0:T(8,128)}), f32[788,768]{1,0:T(8,128)}) %all-reduce.8.cloned.1.call-update) | async-done | bytes 2420752 | tf_op jit(solution)/shard_map/psum | solution.py:114
  664.5 47.5 %all-gather.9 = bf16[1,768,8]{2,0,1:T(2,128)(2,1)S(1)} all-gather(bf16[1,192,8]{2,0,1:T(2,128)(2,1)S(1)} %copy.522), channel_id=11, replica_groups=mesh['fsdp'=4,'expert'=2,'tensor'=4] {'fsdp'}, dimensions={1}, use_global_device_ids=true | all-gather | bytes 15360 | tf_op jit(solution)/shard_map/all_gather | solution.py:88
  726.5 19.9 %scatter_custom_fusion.2 = bf16[2368,768]{1,0:T(8,128)(2,1)} fusion(s32[1576]{0:T(1024)} %copy-done.90, f32[1576,768]{1,0:T(8,128)} %mul.467, f32[1576]{0:T(1024)S(1)} %mul.464, bf16[]{:T(256)} %constant.47.clone.1), kind=kCustom, calls=%fused_computation.104 | custom fusion | flops 2420736 | bytes 8485536 | tf_op jit(solution)/shard_map/scatter | solution.py:216
  751.0 21.4 %multiply_convert_fusion = (bf16[2368,768]{1,0:T(8,128)(2,1)}, f32[2368,768]{1,0:T(8,128)}, f32[2368,768]{1,0:T(8,128)}) fusion(bf16[2368,768]{1,0:T(8,128)(2,1)} %bitcast.29, bf16[2,1,768,768]{3,2,1,0:T(8,128)(2,1)} %param.18), kind=kOutput, calls=%fused_computation.14 | convolution fusion | flops 2911617024 | bytes 23003136 | tf_op jit(solution)/shard_map/dot_general | solution.py:131
  772.4 21.7 %all-to-all-done.4 = bf16[8,296,768]{2,1,0:T(8,128)(2,1)} async-done(((bf16[8,296,768]{2,1,0:T(8,128)(2,1)}), bf16[8,296,768]{2,1,0:T(8,128)(2,1)}, u32[]{:S(2)}, u32[]{:S(2)}) %all-to-all-start.4) | async-done | bytes 3637280 | tf_op jit(solution)/shard_map/all_to_all | solution.py:49
  821.3 57.9 %reduce-scatter.24.cloned.1.call-done = bf16[2368,192]{0,1:T(8,128)(2,1)} async-done(((bf16[2368,768]{0,1:T(8,128)(2,1)}), bf16[2368,192]{0,1:T(8,128)(2,1)}) %reduce-scatter.24.cloned.1.call-update) | async-done | bytes 909328 | tf_op jit(solution)/shard_map/reduce_scatter | solution.py:231
  883.9 20.3 %all_to_all.41 = bf16[8,296,192]{1,2,0:T(8,128)(2,1)} all-to-all(bf16[8,296,192]{1,2,0:T(8,128)(2,1)S(1)} %copy.449), channel_id=1, replica_groups=mesh['fsdp'=4,'expert'=2,'tensor'=4] {'fsdp','expert'}, dimensions={0} | all-to-all | bytes 1818624 | tf_op jit(solution)/shard_map/all_to_all | solution.py:49
  920.4 91.3 %reduce-scatter.22.cloned.1.call-done = f32[2368,192]{0,1:T(8,128)} async-done(((f32[2368,768]{0,1:T(8,128)}), f32[2368,192]{0,1:T(8,128)}) %reduce-scatter.22.cloned.1.call-update) | async-done | bytes 1818640 | tf_op jit(solution)/shard_map/reduce_scatter | solution.py:134
  1064.3 14.0 all-gather.10
  1115.9 56.2 %all-reduce.10.cloned.1.call-done = bf16[788,768]{1,0:T(8,128)(2,1)} async-done(((bf16[788,768]{1,0:T(8,128)(2,1)}), bf16[788,768]{1,0:T(8,128)(2,1)}) %all-reduce.10.cloned.1.call-update) | async-done | bytes 1210384 | tf_op jit(solution)/shard_map/psum | solution.py:293
  1189.6 19.8 %scatter_custom_fusion.3 = bf16[2368,768]{1,0:T(8,128)(2,1)} fusion(s32[1576]{0:T(1024)} %copy-done.90, f32[1576,768]{1,0:T(8,128)} %mul.501, f32[1576]{0:T(1024)S(1)} %mul.498, bf16[]{:T(256)} %constant.47.clone.1), kind=kCustom, calls=%fused_computation.105 | custom fusion | flops 2420736 | bytes 8485536 | tf_op jit(solution)/shard_map/scatter | solution.py:216
  1209.4 47.3 %all_to_all.42 = bf16[8,296,768]{2,1,0:T(8,128)(2,1)S(1)} all-to-all(bf16[8,296,768]{2,1,0:T(8,128)(2,1)} %bitcast.295), channel_id=1, replica_groups=mesh['fsdp'=4,'expert'=2,'tensor'=4] {'fsdp','expert'}, dimensions={0} | all-to-all | bytes 7274496 | tf_op jit(solution)/shard_map/all_to_all | solution.py:49
  1280.4 59.6 %reduce-scatter.26.cloned.1.call-done = bf16[2368,192]{0,1:T(8,128)(2,1)} async-done(((bf16[2368,768]{0,1:T(8,128)(2,1)}), bf16[2368,192]{0,1:T(8,128)(2,1)}) %reduce-scatter.26.cloned.1.call-update) | async-done | bytes 909328 | tf_op jit(solution)/shard_map/reduce_scatter | solution.py:231
  1465.5 41.3 %all-reduce.12.cloned.1.call-done = bf16[788,768]{1,0:T(8,128)(2,1)} async-done(((bf16[788,768]{1,0:T(8,128)(2,1)}), bf16[788,768]{1,0:T(8,128)(2,1)}) %all-reduce.12.cloned.1.call-update) | async-done | bytes 1210384 | tf_op jit(solution)/shard_map/psum | solution.py:293
  1557.6 23.3 %reduce-scatter.28.cloned.1.call-done = bf16[96,4]{1,0:T(8,128)(2,1)} async-done(((bf16[768,4]{1,0:T(8,128)(2,1)}), bf16[96,4]{1,0:T(8,128)(2,1)}) %reduce-scatter.28.cloned.1.call-update) | async-done | bytes 784
  1584.3 33.0 %reduce-scatter.30.cloned.1.call-done = bf16[96,4]{1,0:T(8,128)(2,1)} async-done(((bf16[768,4]{1,0:T(8,128)(2,1)}), bf16[96,4]{1,0:T(8,128)(2,1)}) %reduce-scatter.30.cloned.1.call-update) | async-done | bytes 784
  1620.7 39.6 %reduce-scatter.32.cloned.1.call-done = bf16[96,1152]{1,0:T(8,128)(2,1)} async-done(((bf16[768,1152]{1,0:T(8,128)(2,1)}), bf16[96,1152]{1,0:T(8,128)(2,1)}) %reduce-scatter.32.cloned.1.call-update) | async-done | bytes 221200
  (535 shorter events, 619.4 us)
Async XLA Ops:
  7.2 174.3 %all-reduce.6.cloned.1.call-start = ((), (), s32[]{:S(2)}) async-start(), calls=%async_computation.17 | async-start | bytes 4866048 | tf_op jit(solution)/shard_map/psum | solution.py:114
  28.6 155.8 %copy-start.83 = (f32[768]{0:T(1024)}, f32[768]{0:T(1024)S(1)}, u32[]{:S(2)}) copy-start(f32[768]{0:T(1024)S(1)} %get-tuple-element.92) | copy-start | bytes 9220
  82.6 326.7 %reduce-scatter.20.cloned.1.call-start = ((), (), s32[]{:S(2)}) async-start(), calls=%async_computation.18 | async-start | bytes 9338880 | tf_op jit(solution)/shard_map/reduce_scatter | solution.py:134
  183.8 338.4 %copy-start.4 = (f32[788,768]{1,0:T(8,128)}, f32[788,768]{1,0:T(8,128)S(1)}, u32[]{:S(2)}) copy-start(f32[788,768]{1,0:T(8,128)S(1)} %get-tuple-element.107) | copy-start | bytes 7262212
  415.7 21.1 %all-to-all-start.1 = ((bf16[8,296,192]{1,2,0:T(8,128)(2,1)}), bf16[8,296,192]{1,2,0:T(8,128)(2,1)}, u32[]{:S(2)}, u32[]{:S(2)}) async-start(bf16[8,296,192]{1,2,0:T(8,128)(2,1)} %copy.425), calls=%async_computation.2 | async-start | bytes 2359296 | tf_op jit(solution)/shard_map/all_to_all | solution.py:49
  419.9 99.8 %all-gather.17.cloned.1.call-start = ((), (), s32[]{:S(2)}) async-start(), calls=%async_computation.19 | async-start | bytes 1720320 | tf_op jit(solution)/shard_map/all_gather | solution.py:140
  455.2 176.4 %all-reduce.8.cloned.1.call-start = ((), (), s32[]{:S(2)}) async-start(), calls=%async_computation.20 | async-start | bytes 4866048 | tf_op jit(solution)/shard_map/psum | solution.py:114
  659.8 86.6 %all-to-all-start.2 = ((bf16[8,296,768]{2,1,0:T(8,128)(2,1)}), bf16[8,296,768]{2,1,0:T(8,128)(2,1)}, u32[]{:S(2)}, u32[]{:S(2)}) async-start(bf16[8,296,768]{2,1,0:T(8,128)(2,1)} %bitcast.293), calls=%async_computation.3 | async-start | bytes 7274496 | tf_op jit(solution)/shard_map/all_to_all | solution.py:49
  746.4 47.7 %all-to-all-start.4 = ((bf16[8,296,768]{2,1,0:T(8,128)(2,1)}), bf16[8,296,768]{2,1,0:T(8,128)(2,1)}, u32[]{:S(2)}, u32[]{:S(2)}) async-start(bf16[8,296,768]{2,1,0:T(8,128)(2,1)} %bitcast.294), calls=%async_computation.6 | async-start | bytes 7274496 | tf_op jit(solution)/shard_map/all_to_all | solution.py:49
  750.9 128.2 %reduce-scatter.24.cloned.1.call-start = ((), (), s32[]{:S(2)}) async-start(), calls=%async_computation.23 | async-start | bytes 4669440 | tf_op jit(solution)/shard_map/reduce_scatter | solution.py:231
  812.3 199.4 %reduce-scatter.22.cloned.1.call-start = ((), (), s32[]{:S(2)}) async-start(), calls=%async_computation.21 | async-start | bytes 9338880 | tf_op jit(solution)/shard_map/reduce_scatter | solution.py:134
  821.2 240.5 %all-gather.21.cloned.1.call-start = ((), (), s32[]{:S(2)}) async-start(), calls=%async_computation.24 | async-start | bytes 1720320 | tf_op jit(solution)/shard_map/all_gather | solution.py:240
  1018.1 21.1 %all-to-all-start.3 = ((bf16[8,296,192]{1,2,0:T(8,128)(2,1)}), bf16[8,296,192]{1,2,0:T(8,128)(2,1)}, u32[]{:S(2)}, u32[]{:S(2)}) async-start(bf16[8,296,192]{1,2,0:T(8,128)(2,1)} %copy.444), calls=%async_computation.5 | async-start | bytes 2359296 | tf_op jit(solution)/shard_map/all_to_all | solution.py:49
  1022.3 72.2 %all-gather.19.cloned.1.call-start = ((), (), s32[]{:S(2)}) async-start(), calls=%async_computation.22 | async-start | bytes 1720320 | tf_op jit(solution)/shard_map/all_gather | solution.py:140
  1061.6 110.5 %all-reduce.10.cloned.1.call-start = ((), (), s32[]{:S(2)}) async-start(), calls=%async_computation.25 | async-start | bytes 2433024 | tf_op jit(solution)/shard_map/psum | solution.py:293
  1115.4 224.5 %reduce-scatter.26.cloned.1.call-start = ((), (), s32[]{:S(2)}) async-start(), calls=%async_computation.26 | async-start | bytes 4669440 | tf_op jit(solution)/shard_map/reduce_scatter | solution.py:231
  1343.6 20.5 %all-to-all-start.7 = ((bf16[8,296,192]{1,2,0:T(8,128)(2,1)}), bf16[8,296,192]{1,2,0:T(8,128)(2,1)S(1)}, u32[]{:S(2)}, u32[]{:S(2)}) async-start(bf16[8,296,192]{1,2,0:T(8,128)(2,1)} %copy.463), calls=%async_computation.11 | async-start | bytes 2359296 | tf_op jit(solution)/shard_map/all_to_all | solution.py:49
  1347.3 63.8 %all-gather.23.cloned.1.call-start = ((), (), s32[]{:S(2)}) async-start(), calls=%async_computation.27 | async-start | bytes 1720320 | tf_op jit(solution)/shard_map/all_gather | solution.py:240
  1378.3 68.5 %reduce-scatter.36.cloned.1.call-start = ((), (), s32[]{:S(2)}) async-start(), calls=%async_computation.33 | async-start | bytes 221184
  1403.9 102.9 %all-reduce.12.cloned.1.call-start = ((), (), s32[]{:S(2)}) async-start(), calls=%async_computation.28 | async-start | bytes 2433024 | tf_op jit(solution)/shard_map/psum | solution.py:293
  1430.1 120.3 %reduce-scatter.34.cloned.1.call-start = ((), (), s32[]{:S(2)}) async-start(), calls=%async_computation.32 | async-start | bytes 663552
  1463.0 117.9 %reduce-scatter.28.cloned.1.call-start = ((), (), s32[]{:S(2)}) async-start(), calls=%async_computation.29 | async-start | bytes 221184
  1514.4 102.9 %reduce-scatter.30.cloned.1.call-start = ((), (), s32[]{:S(2)}) async-start(), calls=%async_computation.30 | async-start | bytes 221184
  1517.5 142.9 %reduce-scatter.32.cloned.1.call-start = ((), (), s32[]{:S(2)}) async-start(), calls=%async_computation.31 | async-start | bytes 1990656
  (100 other events, 1397.1 us)
Sparse Core Ops, SparseCore 0:
  82.7 98.7 all-reduce.5
  282.2 127.0 reduce-scatter.19
  455.3 32.5 all-gather.16
  534.2 97.4 all-reduce.7
  812.4 66.7 reduce-scatter.23
  881.4 130.2 reduce-scatter.21
  1013.3 34.3 all-gather.20
  1061.8 32.6 all-gather.18
  1115.6 56.5 all-reduce.9
  1272.7 67.2 reduce-scatter.25
  1378.4 32.6 all-gather.22
  1414.3 32.4 reduce-scatter.35
  1449.2 57.5 all-reduce.11
  1510.1 33.9 reduce-scatter.33
  1547.3 33.5 reduce-scatter.27
  1583.8 33.5 reduce-scatter.29
  1620.9 39.4 reduce-scatter.31
where the time goes:
time: 1680 us; the launch traced here: 1670 us
  waiting for transfers between devices  799 us (48%)
  blocking collectives  302 us (18%)
  local copies, waits for them, and re-layouts  254 us (15%)
  matrix products  157 us (9%)
  other arithmetic  120 us (7%)
  starting transfers between devices  23.7 us (1%)
    reduce_scatter x2, waiting for transfers between devices, on_device(): lax.psum_scatter(partial_out, 'tensor', scatter_dimension=1, tiled=True)  208 us
    psum x2, waiting for transfers between devices, on_device(): lax.psum(jnp.dot(attended, weight_out, preferred_element_type=jnp.float32...  193 us
    reduce_scatter x2, waiting for transfers between devices, on_device(): lax.psum_scatter(partial_in.astype(jnp.bfloat16), 'tensor', scatter_dimen...  117 us
    all_to_all x3, blocking collectives, move_rows(): lax.all_to_all(buffer, ('fsdp', 'expert'), split_axis=0, concat_axis=0, t...  115 us
    unnamed x22, waiting for transfers between devices  110 us
    psum x2, waiting for transfers between devices, on_device(): lax.psum(jnp.einsum('tcj,dcj->td', grad_mixed, weight_qkv, preferred_elem...  97.5 us
    unnamed x240, local copies, waits for them, and re-layouts  59.4 us
    all_gather x2, blocking collectives, on_device(): lax.all_gather(w_router[layer_idx], 'fsdp', axis=0, tiled=True)  56 us
  transfers between devices with their start and end apart: 22, of which 18 were waited for; matrix products, arithmetic and copies ran while one was open for 16% of the time, Pallas kernels for 0%

commit v1 on v0

v1 whole, which is shorter than its diff:
```python
import jax
import jax.numpy as jnp
from jax import lax
from jax.sharding import PartitionSpec as P

HEAD_DIM = 64
SEQ = 197
ROW_TILE = 16

epsilon = 1e-06


def layer_norm(values, gain_row, bias_row):
    center = values - jnp.mean(values, axis=-1, keepdims=True)
    inverse = lax.rsqrt(jnp.mean(center * center, axis=-1, keepdims=True) + epsilon)
    scaled = center * inverse
    return (scaled * gain_row + bias_row, scaled, inverse)


def norm_back(grad_out, scaled, inverse, gain_row):
    grad_scaled = grad_out * gain_row
    grad_values = inverse * (
        grad_scaled
        - jnp.mean(grad_scaled, axis=-1, keepdims=True)
        - scaled * jnp.mean(grad_scaled * scaled, axis=-1, keepdims=True)
    )
    return (grad_values, jnp.sum(grad_out * scaled, axis=0), jnp.sum(grad_out, axis=0))


def slot_positions(routes_dev, expert_count, capacity):
    onehot = (
        routes_dev[:, :, None] == jnp.arange(expert_count, dtype=jnp.int32)[None, None, :]
    ).astype(jnp.int32)
    per_token = jnp.sum(onehot, axis=1)
    earlier = jnp.cumsum(per_token, axis=0) - per_token
    slots = jnp.sum(earlier[:, None, :] * onehot, axis=-1)
    return routes_dev * capacity + slots


def move_rows(buffer, experts):
    rows, cols = buffer.shape
    moved = lax.all_to_all(
        buffer.reshape(experts, rows // experts, cols),
        ("fsdp", "expert"),
        split_axis=0,
        concat_axis=0,
        tiled=True,
    )
    return moved.reshape(rows, cols)


def plain_dot(left, right):
    return jnp.dot(left, right, preferred_element_type=jnp.float32)


def contract_first(left, right):
    return lax.dot_general(
        left, right, (((0,), (0,)), ((), ())), preferred_element_type=jnp.float32
    )


def contract_last(left, right):
    return lax.dot_general(
        left, right, (((1,), (1,)), ((), ())), preferred_element_type=jnp.float32
    )


def gather_layer(w_qkv_layer, w_out_layer, fsdp_width, tensor_width):
    rows, _, cols = w_qkv_layer.shape
    packed = jnp.concatenate([w_qkv_layer.reshape(rows, 3 * cols), w_out_layer], axis=1)
    full = lax.all_gather(packed, ("fsdp", "tensor"), axis=0, tiled=True)
    full = full.reshape(fsdp_width, tensor_width, rows, 4, cols)
    qkv = full[:, :, :, :3].transpose(0, 2, 3, 1, 4)
    qkv = qkv.reshape(fsdp_width * rows, 3 * tensor_width * cols)
    out = full[:, :, :, 3].transpose(1, 2, 0, 3)
    return qkv, out.reshape(tensor_width * rows, fsdp_width * cols)


def scatter_layer(grad_qkv, grad_out, fsdp_width, tensor_width):
    feat = grad_qkv.shape[0]
    rows, cols = feat // fsdp_width, feat // tensor_width
    qkv = grad_qkv.astype(jnp.bfloat16).reshape(fsdp_width, rows, 3, tensor_width, cols)
    qkv = qkv.transpose(0, 3, 1, 2, 4).reshape(fsdp_width, tensor_width, rows, 3 * cols)
    out = grad_out.astype(jnp.bfloat16).reshape(tensor_width, cols, fsdp_width, rows)
    out = out.transpose(2, 0, 1, 3)
    packed = jnp.concatenate([qkv, out], axis=3).reshape(-1, 4 * cols)
    part = lax.psum_scatter(
        packed, ("fsdp", "tensor"), scatter_dimension=0, tiled=True
    ).astype(jnp.float32)
    part = lax.psum(part, "expert")
    return part[:, : 3 * cols].reshape(rows, 3, cols), part[:, 3 * cols :]


def on_device(tokens, routes, cotangent, ln_gain, ln_bias, w_qkv, w_out, w_router, w_in, w_back):
    tok_rows, feat = tokens.shape
    top_count = routes.shape[1]
    fsdp_width = lax.axis_size("fsdp")
    experts = lax.axis_size(("fsdp", "expert"))
    tensor_width = lax.axis_size("tensor")
    capacity = (3 * tok_rows * top_count // (2 * experts) + 7) // 8 * 8
    slot_rows = experts * capacity
    images = tok_rows // SEQ
    own_images = images // tensor_width
    padded = (SEQ + ROW_TILE - 1) // ROW_TILE * ROW_TILE
    own_rows = own_images * padded
    heads = feat // HEAD_DIM
    scale_factor = HEAD_DIM ** (-0.5)
    layer_count = w_qkv.shape[0]
    low = jnp.bfloat16
    share = lax.axis_index("tensor")

    def pad_images(array, fill):
        array = array.reshape(images, SEQ, array.shape[1])
        array = jnp.pad(
            array, ((0, 0), (0, padded - SEQ), (0, 0)), constant_values=fill
        )
        return array.reshape(images * padded, array.shape[2])

    def drop_padding(array):
        array = array.reshape(images, padded, array.shape[1])[:, :SEQ]
        return array.reshape(tok_rows, array.shape[2])

    def own_part(array):
        return lax.dynamic_slice_in_dim(array, share * own_rows, own_rows, 0)

    def all_tokens(array):
        return lax.all_gather(array, "tensor", axis=0, tiled=True)

    def sum_own(array):
        return lax.psum_scatter(array, "tensor", scatter_dimension=0, tiled=True)

    weights = [
        gather_layer(w_qkv[layer], w_out[layer], fsdp_width, tensor_width)
        for layer in range(layer_count)
    ]
    local_feat = w_router.shape[1]
    small = jnp.concatenate(
        [
            w_router.transpose(0, 2, 1).reshape(layer_count * experts, local_feat),
            ln_gain.reshape(2 * layer_count, local_feat),
            ln_bias.reshape(2 * layer_count, local_feat),
        ],
        axis=0,
    )
    small = lax.all_gather(small, "fsdp", axis=1, tiled=True)
    router_all = small[: layer_count * experts].reshape(layer_count, experts, feat)
    norms = small[layer_count * experts :].astype(jnp.float32)
    norms = norms.reshape(2, layer_count, 2, feat)

    positions = slot_positions(pad_images(routes, -1), experts, capacity)
    slot_ids = jnp.arange(slot_rows, dtype=jnp.int32)[:, None]
    dispatch = (
        (positions[None, :, 0] == slot_ids) | (positions[None, :, 1] == slot_ids)
    ).astype(low)
    slot_expert = (
        (slot_ids // capacity) == jnp.arange(experts, dtype=jnp.int32)[None, :]
    ).astype(jnp.float32)
    key_bias = jnp.where(jnp.arange(padded) < SEQ, 0.0, -1e30).astype(jnp.float32)

    def split_heads(array):
        array = array.reshape(own_images, padded, heads, HEAD_DIM)
        return array.transpose(0, 2, 1, 3)

    def join_heads(array):
        return array.transpose(0, 2, 1, 3).reshape(own_rows, feat)

    residual = own_part(pad_images(tokens, 0)).astype(jnp.float32)
    kept_layer = []
    for layer in range(layer_count):
        weight_qkv, weight_out = weights[layer]
        router_rows = router_all[layer]
        gain_pair = norms[0, layer]
        bias_pair = norms[1, layer]
        normed, scaled_first, inverse_first = layer_norm(residual, gain_pair[0], bias_pair[0])
        normed = normed.astype(low)
        mixed = plain_dot(normed, weight_qkv).astype(low)
        queries = split_heads(mixed[:, :feat])
        keys_all = split_heads(mixed[:, feat : 2 * feat])
        values_all = split_heads(mixed[:, 2 * feat :])
        scores = (
            jnp.einsum("ihsd,ihtd->ihst", queries, keys_all, preferred_element_type=jnp.float32)
            * scale_factor
            + key_bias
        )
        grown = jnp.exp(scores - jnp.max(scores, axis=-1, keepdims=True))
        probs_full = grown / jnp.sum(grown, axis=-1, keepdims=True)
        probs_low = probs_full.astype(low)
        attended = join_heads(
            jnp.einsum(
                "ihst,ihtd->ihsd", probs_low, values_all, preferred_element_type=jnp.float32
            ).astype(low)
        )
        middle = residual + plain_dot(attended, weight_out)
        routed, scaled_second, inverse_second = layer_norm(middle, gain_pair[1], bias_pair[1])
        routed = routed.astype(low)
        gate_probs = jax.nn.softmax(contract_last(routed, router_rows), axis=-1)
        buffer = plain_dot(dispatch, all_tokens(routed)).astype(low)
        arrived = move_rows(buffer, experts)
        slot_gates = jax.nn.softmax(contract_last(buffer, router_rows), axis=-1)
        slot_combine = jnp.sum(slot_gates * slot_expert, axis=-1, keepdims=True)
        pre_act = plain_dot(arrived, w_in[layer, 0])
        hidden = jax.nn.gelu(pre_act, approximate=False).astype(low)
        partial_out = plain_dot(hidden, w_back[layer, 0]).astype(low)
        returned = move_rows(partial_out, experts)
        weighted = (slot_combine * returned.astype(jnp.float32)).astype(low)
        mixture = sum_own(contract_first(dispatch, weighted).astype(low))
        kept_layer.append(
            (
                normed,
                scaled_first,
                inverse_first,
                queries,
                keys_all,
                values_all,
                probs_full,
                attended,
                routed,
                scaled_second,
                inverse_second,
                gate_probs,
                slot_combine,
                arrived,
                pre_act,
                hidden,
                returned,
            )
        )
        residual = middle + mixture.astype(jnp.float32)
    output = drop_padding(all_tokens(residual.astype(low)))

    grad_all = pad_images(cotangent, 0)
    grad_res = own_part(grad_all).astype(jnp.float32)
    gain_grads = [None] * layer_count
    bias_grads = [None] * layer_count
    router_grads = [None] * layer_count
    qkv_grads = [None] * layer_count
    out_grads = [None] * layer_count
    in_grads = [None] * layer_count
    back_grads = [None] * layer_count
    for layer in reversed(range(layer_count)):
        (
            normed,
            scaled_first,
            inverse_first,
            queries,
            keys_all,
            values_all,
            probs_full,
            attended,
            routed,
            scaled_second,
            inverse_second,
            gate_probs,
            slot_combine,
            arrived,
            pre_act,
            hidden,
            returned,
        ) = kept_layer[layer]
        weight_qkv, weight_out = weights[layer]
        router_rows = router_all[layer]
        gain_pair = norms[0, layer]
        if grad_all is None:
            grad_all = all_tokens(grad_res.astype(low))
        grad_buffer = (slot_combine * plain_dot(dispatch, grad_all)).astype(low)
        grad_slots = move_rows(grad_buffer, experts)
        slot_dots = jnp.sum(
            returned.astype(jnp.float32) * grad_buffer.astype(jnp.float32), axis=-1, keepdims=True
        )
        spread_dots = slot_dots * slot_expert
        dots_high = spread_dots.astype(low)
        dots_low = (spread_dots - dots_high.astype(jnp.float32)).astype(low)
        gate_dots = contract_first(dispatch, jnp.concatenate([dots_high, dots_low], axis=1))
        gate_dots = sum_own(gate_dots[:, :experts] + gate_dots[:, experts:])
        weight_back = w_back[layer, 0]
        weight_in = w_in[layer, 0]
        grad_hidden = contract_last(grad_slots, weight_back)
        _, gelu_pull = jax.vjp(lambda value: jax.nn.gelu(value, approximate=False), pre_act)
        grad_pre = gelu_pull(grad_hidden)[0].astype(low)
        partial_in = contract_last(grad_pre, weight_in).astype(low)
        grad_returned = move_rows(partial_in, experts)
        back_grads[layer] = contract_first(hidden, grad_slots)
        in_grads[layer] = contract_first(arrived, grad_pre)
        grad_routed = sum_own(contract_first(dispatch, grad_returned).astype(low))
        grad_routed = grad_routed.astype(jnp.float32)
        grad_logits = (
            gate_dots - gate_probs * jnp.sum(gate_dots, axis=-1, keepdims=True)
        ).astype(low)
        router_grads[layer] = contract_first(grad_logits, routed)
        grad_routed = grad_routed + plain_dot(grad_logits, router_rows)
        grad_norm_two, gain_two, bias_two = norm_back(
            grad_routed, scaled_second, inverse_second, gain_pair[1]
        )
        grad_middle = grad_res + grad_norm_two
        grad_branch = grad_middle.astype(low)
        out_grads[layer] = contract_first(attended, grad_branch)
        grad_attended = split_heads(contract_last(grad_branch, weight_out).astype(low))
        grad_values = jnp.einsum(
            "ihst,ihsd->ihtd",
            probs_full.astype(low),
            grad_attended,
            preferred_element_type=jnp.float32,
        )
        grad_probs = jnp.einsum(
            "ihsd,ihtd->ihst", grad_attended, values_all, preferred_element_type=jnp.float32
        )
        grad_scores = (
            probs_full * (grad_probs - jnp.sum(probs_full * grad_probs, axis=-1, keepdims=True))
        ).astype(low)
        grad_queries = (
            jnp.einsum(
                "ihst,ihtd->ihsd", grad_scores, keys_all, preferred_element_type=jnp.float32
            )
            * scale_factor
        )
        grad_keys = (
            jnp.einsum("ihst,ihsd->ihtd", grad_scores, queries, preferred_element_type=jnp.float32)
            * scale_factor
        )
        grad_mixed = jnp.concatenate(
            [
                join_heads(grad_queries.astype(low)),
                join_heads(grad_keys.astype(low)),
                join_heads(grad_values.astype(low)),
            ],
            axis=1,
        )
        grad_normed = contract_last(grad_mixed, weight_qkv)
        grad_norm_one, gain_one, bias_one = norm_back(
            grad_normed, scaled_first, inverse_first, gain_pair[0]
        )
        grad_res = grad_middle + grad_norm_one
        grad_all = None
        qkv_grads[layer], out_grads[layer] = scatter_layer(
            contract_first(normed, grad_mixed), out_grads[layer], fsdp_width, tensor_width
        )
        gain_grads[layer] = jnp.stack([gain_one, gain_two], axis=0)
        bias_grads[layer] = jnp.stack([bias_one, bias_two], axis=0)
    grad_tokens = drop_padding(all_tokens(grad_res.astype(low)).astype(jnp.float32))
    small_grads = jnp.concatenate(router_grads + gain_grads + bias_grads, axis=0)
    small_grads = lax.psum(small_grads, ("fsdp", "expert", "tensor"))
    small_grads = lax.dynamic_slice_in_dim(
        small_grads, lax.axis_index("fsdp") * local_feat, local_feat, 1
    )
    split = layer_count * experts
    grad_router = small_grads[:split].reshape(layer_count, experts, local_feat)
    grad_gain = small_grads[split : split + 2 * layer_count]
    grad_bias = small_grads[split + 2 * layer_count :]
    return (
        output,
        grad_tokens,
        grad_gain.reshape(layer_count, 2, local_feat),
        grad_bias.reshape(layer_count, 2, local_feat),
        jnp.stack(qkv_grads),
        jnp.stack(out_grads),
        grad_router.transpose(0, 2, 1),
        jnp.stack(in_grads)[:, None],
        jnp.stack(back_grads)[:, None],
    )


def solution(mesh):
    in_specs = (
        P(("fsdp", "expert"), None),
        P(("fsdp", "expert"), None),
        P(("fsdp", "expert"), None),
        P(None, None, "fsdp"),
        P(None, None, "fsdp"),
        P(None, "fsdp", None, "tensor"),
        P(None, "tensor", "fsdp"),
        P(None, "fsdp", None),
        P(None, ("fsdp", "expert"), None, "tensor"),
        P(None, ("fsdp", "expert"), "tensor", None),
    )
    out_specs = (
        P(("fsdp", "expert"), None),
        P(("fsdp", "expert"), None),
        P(None, None, "fsdp"),
        P(None, None, "fsdp"),
        P(None, "fsdp", None, "tensor"),
        P(None, "tensor", "fsdp"),
        P(None, "fsdp", None),
        P(None, ("fsdp", "expert"), None, "tensor"),
        P(None, ("fsdp", "expert"), "tensor", None),
    )
    return jax.shard_map(
        on_device, mesh=mesh, in_specs=in_specs, out_specs=out_specs, check_vma=False
    )
```

time: 1680 us -> 1440 us (0.86)
  blocking collectives: 302 us -> 156 us
  other arithmetic: 120 us -> 29.5 us
  matrix products: 157 us -> 222 us
  waiting for transfers between devices: 799 us -> 749 us
  local copies, waits for them, and re-layouts: 254 us -> 232 us
    reduce_scatter x4, waiting for transfers between devices: 325 us -> 47.7 us  [sum_own(): return lax.psum_scatter(array, 'tensor', scatter_dimension=0, tiled=True)]
    all_gather x17 -> x1, blocking collectives: 188 us -> 9.69 us  [on_device(): small = lax.all_gather(small, 'fsdp', axis=1, tiled=True)]
    all_gather x4 -> x7, waiting for transfers between devices: 18.2 us -> 194 us  [the longest x5 123 us: all_tokens(): return lax.all_gather(array, 'tensor', axis=0, tiled=True)]
    psum x4 -> x1, waiting for transfers between devices: 291 us -> 123 us  [on_device(): small_grads = lax.psum(small_grads, ('fsdp', 'expert', 'tensor'))]
    all_to_all x5, waiting for transfers between devices: 55.5 us -> 203 us  [move_rows(): lax.all_to_all(buffer.reshape(experts, rows // experts, cols), ('fsdp', '...]
    unnamed x22 -> x20, waiting for transfers between devices: 110 us -> 181 us
    reshape x20 -> x24, local copies, waits for them, and re-layouts: 35.9 us -> 99.3 us  [the longest x4 36.8 us: scatter_layer(): grad_qkv.astype(jnp.bfloat16)]
    transpose x2 -> x9, local copies, waits for them, and re-layouts: 0.62 us -> 40.7 us  [the longest x4 29.9 us: gather_layer(): qkv = full[:, :, :, :3].transpose(0, 2, 3, 1, 4)]
  transfers between devices with their start and end apart: 22 -> 21, of which waited for: 18 -> 15; matrix products, arithmetic and copies ran while one was open for 16% -> 20% of each run, Pallas kernels for 0% -> 0%
where the time goes in v1:
time: 1440 us; the launch traced here: 1430 us
  waiting for transfers between devices  749 us (52%)
  local copies, waits for them, and re-layouts  232 us (16%)
  matrix products  222 us (15%)
  blocking collectives  156 us (11%)
  other arithmetic  29.5 us (2%)
  starting transfers between devices  25.3 us (2%)
  between operations  16.1 us (1%)
    all_to_all x5, waiting for transfers between devices, move_rows(): lax.all_to_all(buffer.reshape(experts, rows // experts, cols), ('fsdp', '...  203 us
    unnamed x20, waiting for transfers between devices  181 us
    all_to_all x3, blocking collectives, move_rows(): lax.all_to_all(buffer.reshape(experts, rows // experts, cols), ('fsdp', '...  139 us
    psum x1, waiting for transfers between devices, on_device(): small_grads = lax.psum(small_grads, ('fsdp', 'expert', 'tensor'))  123 us
    all_gather x5, waiting for transfers between devices, all_tokens(): return lax.all_gather(array, 'tensor', axis=0, tiled=True)  123 us
    dot_general x14, matrix products, plain_dot(): return jnp.dot(left, right, preferred_element_type=jnp.float32)  98.9 us
    all_gather x2, waiting for transfers between devices, gather_layer(): full = lax.all_gather(packed, ('fsdp', 'tensor'), axis=0, tiled=True)  71.6 us
    dot_general x16, matrix products, contract_first(): lax.dot_general(left, right, (((0,), (0,)), ((), ())), preferred_element_...  66.8 us
  transfers between devices with their start and end apart: 21, of which 15 were waited for; matrix products, arithmetic and copies ran while one was open for 20% of the time, Pallas kernels for 0%

profile of v1, /device:TPU:0, one launch (start us, length us, event | category | flops | bytes accessed | tf_op | source)
XLA Modules:
  0.0 1430.3 jit_solution(14909119382688995527)
XLA Ops:
  23.7 71.6 %all-gather.9.cloned.1.call-done = bf16[3072,768]{1,0:T(8,128)(2,1)} async-done(((bf16[192,768]{1,0:T(8,128)(2,1)}), bf16[3072,768]{1,0:T(8,128)(2,1)}) %all-gather.9.cloned.1.call-update) | async-done | bytes 4718608 | tf_op jit(solution)/shard_map/all_gather | solution.py:71
  95.3 12.9 reshape.500
  126.7 11.5 copy.205
  163.4 28.1 %all-gather.11.cloned.1.call-done = bf16[832,768]{1,0:T(8,128)(2,1)} async-done(((bf16[208,768]{1,0:T(8,128)(2,1)}), bf16[832,768]{1,0:T(8,128)(2,1)}) %all-gather.11.cloned.1.call-update) | async-done | bytes 1277968 | tf_op jit(solution)/shard_map/all_gather | solution.py:127
  191.5 17.2 %convolution_convert_fusion.5 = bf16[2368,768]{1,0:T(8,128)(2,1)} fusion(bf16[832,768]{1,0:T(8,128)(2,1)} %all-gather.11.cloned.1.call-done, s32[832]{0:T(1024)S(1)} %get-tuple-element.88, s32[832]{0:T(1024)S(1)} %get-tuple-element.87), kind=kOutput, calls=%fused_computation.56 | convolution fusion | flops 3033919488 | bytes 4921856 | tf_op jit(solution)/shard_map/dot_general | solution.py:53
  214.8 48.2 %all-to-all-done = bf16[8,296,768]{2,1,0:T(8,128)(2,1)} async-done(((bf16[8,296,768]{2,1,0:T(8,128)(2,1)}), bf16[8,296,768]{2,1,0:T(8,128)(2,1)}, u32[]{:S(2)}, u32[]{:S(2)}) %all-to-all-start) | async-done | bytes 3637280 | tf_op jit(solution)/shard_map/all_to_all | solution.py:42
  263.0 20.7 %multiply_convert_fusion.3 = (bf16[2368,768]{1,0:T(8,128)(2,1)S(1)}, f32[2368,768]{1,0:T(8,128)}, f32[2368,768]{1,0:T(8,128)}) fusion(bf16[2368,768]{1,0:T(8,128)(2,1)} %bitcast.28, bf16[2,1,768,768]{3,2,1,0:T(8,128)(2,1)S(1)} %copy-done.95), kind=kOutput, calls=%fused_computation.34 | convolution fusion | flops 2911617024 | bytes 23003136 | tf_op jit(solution)/shard_map/dot_general | solution.py:53
  296.0 40.3 %all-to-all-done.1 = bf16[8,296,768]{2,1,0:T(8,128)(2,1)} async-done(((bf16[8,296,768]{2,1,0:T(8,128)(2,1)}), bf16[8,296,768]{2,1,0:T(8,128)(2,1)}, u32[]{:S(2)}, u32[]{:S(2)}) %all-to-all-start.1) | async-done | bytes 3637280 | tf_op jit(solution)/shard_map/all_to_all | solution.py:42
  344.1 12.9 reshape.517
  402.4 31.4 %all-gather.15.cloned.1.call-done = bf16[832,768]{1,0:T(8,128)(2,1)} async-done(((bf16[208,768]{1,0:T(8,128)(2,1)}), bf16[832,768]{1,0:T(8,128)(2,1)}) %all-gather.15.cloned.1.call-update) | async-done | bytes 1277968 | tf_op jit(solution)/shard_map/all_gather | solution.py:127
  439.9 46.8 %all_to_all.40 = bf16[8,296,768]{2,1,0:T(8,128)(2,1)S(1)} all-to-all(bf16[8,296,768]{2,1,0:T(8,128)(2,1)S(1)} %bitcast.278), channel_id=1, replica_groups=mesh['fsdp'=4,'expert'=2,'tensor'=4] {'fsdp','expert'}, dimensions={0} | all-to-all | bytes 7274496 | tf_op jit(solution)/shard_map/all_to_all | solution.py:42
  486.7 19.2 %multiply_convert_fusion.2 = (bf16[2368,768]{1,0:T(8,128)(2,1)S(1)}, f32[2368,768]{1,0:T(8,128)}, f32[2368,768]{1,0:T(8,128)}) fusion(bf16[2368,768]{1,0:T(8,128)(2,1)S(1)} %bitcast.292, bf16[2,1,768,768]{3,2,1,0:T(8,128)(2,1)S(1)} %copy-done.96), kind=kOutput, calls=%fused_computation.21 | convolution fusion | flops 2911617024 | bytes 23003136 | tf_op jit(solution)/shard_map/dot_general | solution.py:53
  523.4 34.9 %all-to-all-done.3 = bf16[8,296,768]{2,1,0:T(8,128)(2,1)} async-done(((bf16[8,296,768]{2,1,0:T(8,128)(2,1)}), bf16[8,296,768]{2,1,0:T(8,128)(2,1)}, u32[]{:S(2)}, u32[]{:S(2)}) %all-to-all-start.3) | async-done | bytes 3637280 | tf_op jit(solution)/shard_map/all_to_all | solution.py:42
  566.0 45.7 %all_to_all.41 = bf16[8,296,768]{2,1,0:T(8,128)(2,1)S(1)} all-to-all(bf16[8,296,768]{2,1,0:T(8,128)(2,1)S(1)} %bitcast.303), channel_id=1, replica_groups=mesh['fsdp'=4,'expert'=2,'tensor'=4] {'fsdp','expert'}, dimensions={0} | all-to-all | bytes 7274496 | tf_op jit(solution)/shard_map/all_to_all | solution.py:42
  633.4 39.8 %all-to-all-done.5 = bf16[8,296,768]{2,1,0:T(8,128)(2,1)} async-done(((bf16[8,296,768]{2,1,0:T(8,128)(2,1)}), bf16[8,296,768]{2,1,0:T(8,128)(2,1)}, u32[]{:S(2)}, u32[]{:S(2)}) %all-to-all-start.5) | async-done | bytes 3637280 | tf_op jit(solution)/shard_map/all_to_all | solution.py:42
  690.6 17.9 %reduce-scatter.21.cloned.1.call-done = bf16[208,768]{1,0:T(8,128)(2,1)} async-done(((bf16[832,768]{1,0:T(8,128)(2,1)}), bf16[208,768]{1,0:T(8,128)(2,1)}) %reduce-scatter.21.cloned.1.call-update) | async-done | bytes 319504 | tf_op jit(solution)/shard_map/reduce_scatter | solution.py:130
  711.4 29.7 %reduce-scatter.19.cloned.1.call-done = bf16[208,768]{1,0:T(8,128)(2,1)} async-done(((bf16[832,768]{1,0:T(8,128)(2,1)}), bf16[208,768]{1,0:T(8,128)(2,1)}) %reduce-scatter.19.cloned.1.call-update) | async-done | bytes 319504 | tf_op jit(solution)/shard_map/reduce_scatter | solution.py:130
  753.6 31.1 %all-gather.19.cloned.1.call-done = bf16[832,768]{1,0:T(8,128)(2,1)} async-done(((bf16[208,768]{1,0:T(8,128)(2,1)}), bf16[832,768]{1,0:T(8,128)(2,1)}) %all-gather.19.cloned.1.call-update) | async-done | bytes 1277968 | tf_op jit(solution)/shard_map/all_gather | solution.py:127
  792.4 46.7 %all_to_all.42 = bf16[8,296,768]{2,1,0:T(8,128)(2,1)S(1)} all-to-all(bf16[8,296,768]{2,1,0:T(8,128)(2,1)S(1)} %bitcast.302), channel_id=1, replica_groups=mesh['fsdp'=4,'expert'=2,'tensor'=4] {'fsdp','expert'}, dimensions={0} | all-to-all | bytes 7274496 | tf_op jit(solution)/shard_map/all_to_all | solution.py:42
  860.6 40.0 %all-to-all-done.7 = bf16[8,296,768]{2,1,0:T(8,128)(2,1)} async-done(((bf16[8,296,768]{2,1,0:T(8,128)(2,1)}), bf16[8,296,768]{2,1,0:T(8,128)(2,1)}, u32[]{:S(2)}, u32[]{:S(2)}) %all-to-all-start.7) | async-done | bytes 3637280 | tf_op jit(solution)/shard_map/all_to_all | solution.py:42
  1069.3 41.0 %reduce-scatter.31.cloned.1.call-done = bf16[192,768]{1,0:T(8,128)(2,1)} async-done(((bf16[3072,768]{1,0:T(8,128)(2,1)}), bf16[192,768]{1,0:T(8,128)(2,1)}) %reduce-scatter.31.cloned.1.call-update) | async-done | bytes 294928
  1111.4 122.7 %all-reduce.8.cloned.1.call-done = f32[24,768]{1,0:T(8,128)} async-done(((f32[24,768]{1,0:T(8,128)}), f32[24,768]{1,0:T(8,128)}) %all-reduce.8.cloned.1.call-update) | async-done | bytes 73744 | tf_op jit(solution)/shard_map/psum | solution.py:341
  1237.6 32.0 %all-gather.21.cloned.1.call-done = bf16[832,768]{1,0:T(8,128)(2,1)} async-done(((bf16[208,768]{1,0:T(8,128)(2,1)}), bf16[832,768]{1,0:T(8,128)(2,1)}) %all-gather.21.cloned.1.call-update) | async-done | bytes 1277968 | tf_op jit(solution)/shard_map/all_gather | solution.py:127
  1272.8 139.6 %reduce-scatter.29.cloned.1.call-done = bf16[192,768]{1,0:T(8,128)(2,1)} async-done(((bf16[3072,768]{1,0:T(8,128)(2,1)}), bf16[192,768]{1,0:T(8,128)(2,1)}) %reduce-scatter.29.cloned.1.call-update) | async-done | bytes 294928
  (470 shorter events, 432.2 us)
Async XLA Ops:
  7.2 88.1 %all-gather.9.cloned.1.call-start = ((), (), s32[]{:S(2)}) async-start(), calls=%async_computation.16 | async-start | bytes 5013504 | tf_op jit(solution)/shard_map/all_gather | solution.py:71
  12.0 179.5 %all-gather.11.cloned.1.call-start = ((), (), s32[]{:S(2)}) async-start(), calls=%async_computation.17 | async-start | bytes 1597440 | tf_op jit(solution)/shard_map/all_gather | solution.py:127
  21.9 270.8 %copy-start.46 = (bf16[768,24]{0,1:T(8,128)(2,1)}, bf16[768,24]{0,1:T(8,128)(2,1)S(1)}, u32[]{:S(2)}) copy-start(bf16[768,24]{0,1:T(8,128)(2,1)S(1)} %reshape.569) | copy-start | bytes 110596
  22.7 368.9 %copy-start.52 = (f32[768]{0:T(1024)}, f32[768]{0:T(1024)S(1)}, u32[]{:S(2)}) copy-start(f32[768]{0:T(1024)S(1)} %get-tuple-element.82) | copy-start | bytes 9220
  22.7 368.9 %copy-start.61 = (f32[768]{0:T(1024)}, f32[768]{0:T(1024)S(1)}, u32[]{:S(2)}) copy-start(f32[768]{0:T(1024)S(1)} %get-tuple-element.81) | copy-start | bytes 9220
  208.7 54.3 %all-to-all-start = ((bf16[8,296,768]{2,1,0:T(8,128)(2,1)}), bf16[8,296,768]{2,1,0:T(8,128)(2,1)}, u32[]{:S(2)}, u32[]{:S(2)}) async-start(bf16[8,296,768]{2,1,0:T(8,128)(2,1)} %bitcast.277), calls=%async_computation | async-start | bytes 7274496 | tf_op jit(solution)/shard_map/all_to_all | solution.py:42
  213.4 130.7 %all-gather.13.cloned.1.call-start = ((), (), s32[]{:S(2)}) async-start(), calls=%async_computation.19 | async-start | bytes 5013504 | tf_op jit(solution)/shard_map/all_gather | solution.py:71
  288.2 48.1 %all-to-all-start.1 = ((bf16[8,296,768]{2,1,0:T(8,128)(2,1)}), bf16[8,296,768]{2,1,0:T(8,128)(2,1)}, u32[]{:S(2)}, u32[]{:S(2)}) async-start(bf16[8,296,768]{2,1,0:T(8,128)(2,1)} %bitcast.301), calls=%async_computation.1 | async-start | bytes 7274496 | tf_op jit(solution)/shard_map/all_to_all | solution.py:42
  292.7 97.5 %reduce-scatter.17.cloned.1.call-start = ((), (), s32[]{:S(2)}) async-start(), calls=%async_computation.18 | async-start | bytes 1597440 | tf_op jit(solution)/shard_map/reduce_scatter | solution.py:130
  343.8 89.9 %all-gather.15.cloned.1.call-start = ((), (), s32[]{:S(2)}) async-start(), calls=%async_computation.20 | async-start | bytes 1597440 | tf_op jit(solution)/shard_map/all_gather | solution.py:127
  510.4 47.9 %all-to-all-start.3 = ((bf16[8,296,768]{2,1,0:T(8,128)(2,1)}), bf16[8,296,768]{2,1,0:T(8,128)(2,1)}, u32[]{:S(2)}, u32[]{:S(2)}) async-start(bf16[8,296,768]{2,1,0:T(8,128)(2,1)} %bitcast.300), calls=%async_computation.4 | async-start | bytes 7274496 | tf_op jit(solution)/shard_map/all_to_all | solution.py:42
  625.6 47.7 %all-to-all-start.5 = ((bf16[8,296,768]{2,1,0:T(8,128)(2,1)}), bf16[8,296,768]{2,1,0:T(8,128)(2,1)}, u32[]{:S(2)}, u32[]{:S(2)}) async-start(bf16[8,296,768]{2,1,0:T(8,128)(2,1)} %bitcast.299), calls=%async_computation.7 | async-start | bytes 7274496 | tf_op jit(solution)/shard_map/all_to_all | solution.py:42
  630.1 58.5 %reduce-scatter.25.cloned.1.call-start = ((), (), s32[]{:S(2)}) async-start(), calls=%async_computation.28 | async-start | bytes 532480
  633.0 75.5 %reduce-scatter.21.cloned.1.call-start = ((), (), s32[]{:S(2)}) async-start(), calls=%async_computation.23 | async-start | bytes 1597440 | tf_op jit(solution)/shard_map/reduce_scatter | solution.py:130
  680.4 60.6 %reduce-scatter.19.cloned.1.call-start = ((), (), s32[]{:S(2)}) async-start(), calls=%async_computation.21 | async-start | bytes 1597440 | tf_op jit(solution)/shard_map/reduce_scatter | solution.py:130
  688.1 96.6 %all-gather.19.cloned.1.call-start = ((), (), s32[]{:S(2)}) async-start(), calls=%async_computation.24 | async-start | bytes 1597440 | tf_op jit(solution)/shard_map/all_gather | solution.py:127
  852.9 47.7 %all-to-all-start.7 = ((bf16[8,296,768]{2,1,0:T(8,128)(2,1)}), bf16[8,296,768]{2,1,0:T(8,128)(2,1)}, u32[]{:S(2)}, u32[]{:S(2)}) async-start(bf16[8,296,768]{2,1,0:T(8,128)(2,1)} %bitcast.298), calls=%async_computation.10 | async-start | bytes 7274496 | tf_op jit(solution)/shard_map/all_to_all | solution.py:42
  857.5 110.7 %reduce-scatter.27.cloned.1.call-start = ((), (), s32[]{:S(2)}) async-start(), calls=%async_computation.29 | async-start | bytes 532480
  860.6 110.4 %reduce-scatter.23.cloned.1.call-start = ((), (), s32[]{:S(2)}) async-start(), calls=%async_computation.25 | async-start | bytes 1597440 | tf_op jit(solution)/shard_map/reduce_scatter | solution.py:130
  907.9 141.2 %all-gather.17.cloned.1.call-start = ((), (), s32[]{:S(2)}) async-start(), calls=%async_computation.22 | async-start | bytes 1597440 | tf_op jit(solution)/shard_map/all_gather | solution.py:127
  908.4 201.8 %reduce-scatter.31.cloned.1.call-start = ((), (), s32[]{:S(2)}) async-start(), calls=%async_computation.31 | async-start | bytes 5013504
  964.5 269.6 %all-reduce.8.cloned.1.call-start = ((), (), s32[]{:S(2)}) async-start(), calls=%async_computation.27 | async-start | bytes 147456 | tf_op jit(solution)/shard_map/psum | solution.py:341
  985.7 284.0 %all-gather.21.cloned.1.call-start = ((), (), s32[]{:S(2)}) async-start(), calls=%async_computation.26 | async-start | bytes 1597440 | tf_op jit(solution)/shard_map/all_gather | solution.py:127
  986.7 425.7 %reduce-scatter.29.cloned.1.call-start = ((), (), s32[]{:S(2)}) async-start(), calls=%async_computation.30 | async-start | bytes 5013504
  (106 other events, 1591.1 us)
Sparse Core Ops, SparseCore 0:
  12.1 83.1 all-gather.8
  160.6 30.7 all-gather.10
  217.6 91.7 all-gather.12
  343.9 29.7 reduce-scatter.16
  402.5 31.2 all-gather.14
  633.6 20.3 reduce-scatter.24
  680.6 27.9 reduce-scatter.20
  711.6 29.4 reduce-scatter.18
  753.7 30.9 all-gather.18
  860.7 20.2 reduce-scatter.26
  908.0 27.9 reduce-scatter.22
  937.4 30.9 all-gather.16
  973.5 136.7 reduce-scatter.30
  1116.6 117.4 all-reduce.7
  1235.6 33.9 all-gather.20
  1275.5 136.8 reduce-scatter.28

commit v2 on v1

--- a/solution.py
+++ b/solution.py
@@ -65,36 +65,68 @@
     )
 
 
-def gather_layer(w_qkv_layer, w_out_layer, fsdp_width, tensor_width):
+def swap_cores(array):
+    width = lax.axis_size("expert")
+    pairs = [(core, width - 1 - core) for core in range(width)]
+    return lax.ppermute(array, "expert", pairs)
+
+
+def gather_layer(w_qkv_layer, w_out_layer):
     rows, _, cols = w_qkv_layer.shape
-    packed = jnp.concatenate([w_qkv_layer.reshape(rows, 3 * cols), w_out_layer], axis=1)
-    full = lax.all_gather(packed, ("fsdp", "tensor"), axis=0, tiled=True)
-    full = full.reshape(fsdp_width, tensor_width, rows, 4, cols)
-    qkv = full[:, :, :, :3].transpose(0, 2, 3, 1, 4)
-    qkv = qkv.reshape(fsdp_width * rows, 3 * tensor_width * cols)
-    out = full[:, :, :, 3].transpose(1, 2, 0, 3)
-    return qkv, out.reshape(tensor_width * rows, fsdp_width * cols)
-
-
-def scatter_layer(grad_qkv, grad_out, fsdp_width, tensor_width):
-    feat = grad_qkv.shape[0]
-    rows, cols = feat // fsdp_width, feat // tensor_width
-    qkv = grad_qkv.astype(jnp.bfloat16).reshape(fsdp_width, rows, 3, tensor_width, cols)
-    qkv = qkv.transpose(0, 3, 1, 2, 4).reshape(fsdp_width, tensor_width, rows, 3 * cols)
-    out = grad_out.astype(jnp.bfloat16).reshape(tensor_width, cols, fsdp_width, rows)
-    out = out.transpose(2, 0, 1, 3)
-    packed = jnp.concatenate([qkv, out], axis=3).reshape(-1, 4 * cols)
+    packed = jnp.concatenate(
+        [w_qkv_layer.reshape(rows, 3 * cols), w_out_layer.transpose(1, 0)], axis=1
+    )
+    tensor_width = lax.axis_size("tensor")
+    full = lax.all_gather(packed, ("tensor", "fsdp"), axis=0, tiled=True)
+    return full.reshape(tensor_width, -1, 4 * cols)
+
+
+def scatter_layer(grad_packed, small_grads):
+    tensor_width = lax.axis_size("tensor")
+    fsdp_width = lax.axis_size("fsdp")
+    cores = lax.axis_size("expert")
+    _, feat, cols = grad_packed.shape
+    rows = feat // fsdp_width
+    half = rows // cores
+    small_count = small_grads.shape[0]
+    small = small_grads.reshape(small_count, fsdp_width, rows).transpose(1, 0, 2)
+    small = small.reshape(fsdp_width, small_count * rows)
+    small_rows = (small_count * rows + cols - 1) // cols
+    small_rows = (small_rows + ROW_TILE - 1) // ROW_TILE * ROW_TILE
+    small = jnp.pad(small, ((0, 0), (0, small_rows * cols - small_count * rows)))
+    small = small.astype(jnp.bfloat16).reshape(1, fsdp_width, small_rows, cols)
+    small = jnp.broadcast_to(small, (tensor_width, fsdp_width, small_rows, cols))
+    split = grad_packed.astype(jnp.bfloat16).reshape(
+        tensor_width, fsdp_width, cores, half, cols
+    )
+    core = lax.axis_index("expert")
+    mine = lax.dynamic_index_in_dim(split, core, 2, keepdims=False)
+    theirs = lax.dynamic_index_in_dim(split, 1 - core, 2, keepdims=False)
+    chunk = half + small_rows
+    mine = jnp.concatenate([mine, small], axis=2).reshape(-1, cols)
+    theirs = jnp.concatenate([theirs, small], axis=2).reshape(-1, cols)
+    both = mine.astype(jnp.float32) + swap_cores(theirs).astype(jnp.float32)
     part = lax.psum_scatter(
-        packed, ("fsdp", "tensor"), scatter_dimension=0, tiled=True
+        both.astype(jnp.bfloat16), ("tensor", "fsdp"), scatter_dimension=0, tiled=True
+    )
+    small_sum = part[half:chunk].reshape(-1)[: small_count * rows]
+    own_half = part[:half]
+    other_half = swap_cores(own_half)
+    upper = core == 1
+    whole = jnp.concatenate(
+        [jnp.where(upper, other_half, own_half), jnp.where(upper, own_half, other_half)], axis=0
     ).astype(jnp.float32)
-    part = lax.psum(part, "expert")
-    return part[:, : 3 * cols].reshape(rows, 3, cols), part[:, 3 * cols :]
+    qkv_cols = cols // 4 * 3
+    return (
+        whole[:, :qkv_cols].reshape(rows, 3, qkv_cols // 3),
+        whole[:, qkv_cols:].transpose(1, 0),
+        small_sum.astype(jnp.float32).reshape(small_count, rows),
+    )
 
 
 def on_device(tokens, routes, cotangent, ln_gain, ln_bias, w_qkv, w_out, w_router, w_in, w_back):
     tok_rows, feat = tokens.shape
     top_count = routes.shape[1]
-    fsdp_width = lax.axis_size("fsdp")
     experts = lax.axis_size(("fsdp", "expert"))
     tensor_width = lax.axis_size("tensor")
     capacity = (3 * tok_rows * top_count // (2 * experts) + 7) // 8 * 8
@@ -103,7 +135,8 @@
     own_images = images // tensor_width
     padded = (SEQ + ROW_TILE - 1) // ROW_TILE * ROW_TILE
     own_rows = own_images * padded
-    heads = feat // HEAD_DIM
+    share_cols = feat // tensor_width
+    heads = share_cols // HEAD_DIM
     scale_factor = HEAD_DIM ** (-0.5)
     layer_count = w_qkv.shape[0]
     low = jnp.bfloat16
@@ -130,8 +163,7 @@
         return lax.psum_scatter(array, "tensor", scatter_dimension=0, tiled=True)
 
     weights = [
-        gather_layer(w_qkv[layer], w_out[layer], fsdp_width, tensor_width)
-        for layer in range(layer_count)
+        gather_layer(w_qkv[layer], w_out[layer]) for layer in range(layer_count)
     ]
     local_feat = w_router.shape[1]
     small = jnp.concatenate(
@@ -158,27 +190,28 @@
     key_bias = jnp.where(jnp.arange(padded) < SEQ, 0.0, -1e30).astype(jnp.float32)
 
     def split_heads(array):
-        array = array.reshape(own_images, padded, heads, HEAD_DIM)
-        return array.transpose(0, 2, 1, 3)
+        array = array.reshape(tensor_width, own_images, padded, -1, heads, HEAD_DIM)
+        return array.transpose(3, 0, 1, 4, 2, 5)
 
     def join_heads(array):
-        return array.transpose(0, 2, 1, 3).reshape(own_rows, feat)
+        array = array.transpose(0, 1, 3, 2, 4)
+        return array.reshape(tensor_width, own_rows, share_cols)
 
     residual = own_part(pad_images(tokens, 0)).astype(jnp.float32)
     kept_layer = []
     for layer in range(layer_count):
-        weight_qkv, weight_out = weights[layer]
+        weight = weights[layer]
+        weight_qkv = weight[:, :, : 3 * share_cols]
+        weight_out = weight[:, :, 3 * share_cols :]
         router_rows = router_all[layer]
         gain_pair = norms[0, layer]
         bias_pair = norms[1, layer]
         normed, scaled_first, inverse_first = layer_norm(residual, gain_pair[0], bias_pair[0])
         normed = normed.astype(low)
-        mixed = plain_dot(normed, weight_qkv).astype(low)
-        queries = split_heads(mixed[:, :feat])
-        keys_all = split_heads(mixed[:, feat : 2 * feat])
-        values_all = split_heads(mixed[:, 2 * feat :])
+        mixed = jnp.stack([plain_dot(normed, part) for part in weight_qkv]).astype(low)
+        queries, keys_all, values_all = split_heads(mixed)
         scores = (
-            jnp.einsum("ihsd,ihtd->ihst", queries, keys_all, preferred_element_type=jnp.float32)
+            jnp.einsum("gihsd,gihtd->gihst", queries, keys_all, preferred_element_type=jnp.float32)
             * scale_factor
             + key_bias
         )
@@ -187,10 +220,12 @@
         probs_low = probs_full.astype(low)
         attended = join_heads(
             jnp.einsum(
-                "ihst,ihtd->ihsd", probs_low, values_all, preferred_element_type=jnp.float32
+                "gihst,gihtd->gihsd", probs_low, values_all, preferred_element_type=jnp.float32
             ).astype(low)
         )
-        middle = residual + plain_dot(attended, weight_out)
+        middle = residual
+        for part in range(tensor_width):
+            middle = middle + contract_last(attended[part], weight_out[part])
         routed, scaled_second, inverse_second = layer_norm(middle, gain_pair[1], bias_pair[1])
         routed = routed.astype(low)
         gate_probs = jax.nn.softmax(contract_last(routed, router_rows), axis=-1)
@@ -230,9 +265,7 @@
 
     grad_all = pad_images(cotangent, 0)
     grad_res = own_part(grad_all).astype(jnp.float32)
-    gain_grads = [None] * layer_count
-    bias_grads = [None] * layer_count
-    router_grads = [None] * layer_count
+    small_grads = [None] * layer_count
     qkv_grads = [None] * layer_count
     out_grads = [None] * layer_count
     in_grads = [None] * layer_count
@@ -257,7 +290,9 @@
             hidden,
             returned,
         ) = kept_layer[layer]
-        weight_qkv, weight_out = weights[layer]
+        weight = weights[layer]
+        weight_qkv = weight[:, :, : 3 * share_cols]
+        weight_out = weight[:, :, 3 * share_cols :]
         router_rows = router_all[layer]
         gain_pair = norms[0, layer]
         if grad_all is None:
@@ -286,35 +321,36 @@
         grad_logits = (
             gate_dots - gate_probs * jnp.sum(gate_dots, axis=-1, keepdims=True)
         ).astype(low)
-        router_grads[layer] = contract_first(grad_logits, routed)
+        router_grad = contract_first(grad_logits, routed)
         grad_routed = grad_routed + plain_dot(grad_logits, router_rows)
         grad_norm_two, gain_two, bias_two = norm_back(
             grad_routed, scaled_second, inverse_second, gain_pair[1]
         )
         grad_middle = grad_res + grad_norm_two
         grad_branch = grad_middle.astype(low)
-        out_grads[layer] = contract_first(attended, grad_branch)
-        grad_attended = split_heads(contract_last(grad_branch, weight_out).astype(low))
+        grad_out = jnp.stack([contract_first(grad_branch, part) for part in attended])
+        grad_attended = jnp.stack([plain_dot(grad_branch, part) for part in weight_out])
+        grad_attended = split_heads(grad_attended.astype(low))[0]
         grad_values = jnp.einsum(
-            "ihst,ihsd->ihtd",
+            "gihst,gihsd->gihtd",
             probs_full.astype(low),
             grad_attended,
             preferred_element_type=jnp.float32,
         )
         grad_probs = jnp.einsum(
-            "ihsd,ihtd->ihst", grad_attended, values_all, preferred_element_type=jnp.float32
+            "gihsd,gihtd->gihst", grad_attended, values_all, preferred_element_type=jnp.float32
         )
         grad_scores = (
             probs_full * (grad_probs - jnp.sum(probs_full * grad_probs, axis=-1, keepdims=True))
         ).astype(low)
         grad_queries = (
             jnp.einsum(
-                "ihst,ihtd->ihsd", grad_scores, keys_all, preferred_element_type=jnp.float32
+                "gihst,gihtd->gihsd", grad_scores, keys_all, preferred_element_type=jnp.float32
             )
             * scale_factor
         )
         grad_keys = (
-            jnp.einsum("ihst,ihsd->ihtd", grad_scores, queries, preferred_element_type=jnp.float32)
+            jnp.einsum("gihst,gihsd->gihtd", grad_scores, queries, preferred_element_type=jnp.float32)
             * scale_factor
         )
         grad_mixed = jnp.concatenate(
@@ -323,34 +359,33 @@
                 join_heads(grad_keys.astype(low)),
                 join_heads(grad_values.astype(low)),
             ],
-            axis=1,
-        )
-        grad_normed = contract_last(grad_mixed, weight_qkv)
+            axis=2,
+        )
+        grad_normed = sum(
+            contract_last(grad_mixed[part], weight_qkv[part]) for part in range(tensor_width)
+        )
         grad_norm_one, gain_one, bias_one = norm_back(
             grad_normed, scaled_first, inverse_first, gain_pair[0]
         )
         grad_res = grad_middle + grad_norm_one
         grad_all = None
-        qkv_grads[layer], out_grads[layer] = scatter_layer(
-            contract_first(normed, grad_mixed), out_grads[layer], fsdp_width, tensor_width
-        )
-        gain_grads[layer] = jnp.stack([gain_one, gain_two], axis=0)
-        bias_grads[layer] = jnp.stack([bias_one, bias_two], axis=0)
+        grad_qkv = jnp.stack([contract_first(normed, part) for part in grad_mixed])
+        qkv_grads[layer], out_grads[layer], small_grads[layer] = scatter_layer(
+            jnp.concatenate([grad_qkv.astype(low), grad_out.astype(low)], axis=2),
+            jnp.concatenate(
+                [router_grad, jnp.stack([gain_one, gain_two, bias_one, bias_two])], axis=0
+            ),
+        )
     grad_tokens = drop_padding(all_tokens(grad_res.astype(low)).astype(jnp.float32))
-    small_grads = jnp.concatenate(router_grads + gain_grads + bias_grads, axis=0)
-    small_grads = lax.psum(small_grads, ("fsdp", "expert", "tensor"))
-    small_grads = lax.dynamic_slice_in_dim(
-        small_grads, lax.axis_index("fsdp") * local_feat, local_feat, 1
-    )
-    split = layer_count * experts
-    grad_router = small_grads[:split].reshape(layer_count, experts, local_feat)
-    grad_gain = small_grads[split : split + 2 * layer_count]
-    grad_bias = small_grads[split + 2 * layer_count :]
+    small_all = jnp.stack(small_grads)
+    grad_router = small_all[:, :experts]
+    grad_gain = small_all[:, experts : experts + 2]
+    grad_bias = small_all[:, experts + 2 :]
     return (
         output,
         grad_tokens,
-        grad_gain.reshape(layer_count, 2, local_feat),
-        grad_bias.reshape(layer_count, 2, local_feat),
+        grad_gain,
+        grad_bias,
         jnp.stack(qkv_grads),
         jnp.stack(out_grads),
         grad_router.transpose(0, 2, 1),

time: 1440 us -> 1260 us (0.88)
  local copies, waits for them, and re-layouts: 232 us -> 69.3 us
  blocking collectives: 156 us -> 103 us
  waiting for transfers between devices: 749 us -> 715 us
  matrix products: 222 us -> 255 us
  other arithmetic: 29.5 us -> 57.6 us
    reduce_scatter x0 -> x2, waiting for transfers between devices: none -> 219 us  [scatter_layer(): lax.psum_scatter(both.astype(jnp.bfloat16), ('tensor', 'fsdp'), scatter_d...]
    unnamed x20 -> x17, waiting for transfers between devices: 181 us -> 0.29 us
    psum x1 -> x0, waiting for transfers between devices: 123 us -> none  [on_device(): small_grads = lax.psum(small_grads, ('fsdp', 'expert', 'tensor'))]
    reshape x15 -> x9, local copies, waits for them, and re-layouts: 93.1 us -> 5.94 us  [the longest x6 5.72 us: join_heads(): return array.reshape(tensor_width, own_rows, share_cols)]
    all_to_all x3 -> x2, blocking collectives: 139 us -> 93.1 us  [move_rows(): lax.all_to_all(buffer.reshape(experts, rows // experts, cols), ('fsdp', '...]
    transpose x9 -> x1, local copies, waits for them, and re-layouts: 40.7 us -> 1.59 us  [gather_layer(): w_out_layer.transpose(1, 0)]
    all_to_all x5 -> x6, waiting for transfers between devices: 203 us -> 240 us  [move_rows(): lax.all_to_all(buffer.reshape(experts, rows // experts, cols), ('fsdp', '...]
    dot_general x0 -> x24, local copies, waits for them, and re-layouts: none -> 35.3 us  [the longest x20 34.6 us: plain_dot(): return jnp.dot(left, right, preferred_element_type=jnp.float32)]
  transfers between devices with their start and end apart: 21 -> 25, of which waited for: 15 -> 19; matrix products, arithmetic and copies ran while one was open for 20% -> 17% of each run, Pallas kernels for 0% -> 0%
where the time goes in v2:
time: 1260 us; the launch traced here: 1250 us
  waiting for transfers between devices  715 us (57%)
  matrix products  255 us (20%)
  blocking collectives  103 us (8%)
  local copies, waits for them, and re-layouts  69.3 us (6%)
  other arithmetic  57.6 us (5%)
  starting transfers between devices  30.3 us (2%)
  between operations  16.4 us (1%)
    all_to_all x6, waiting for transfers between devices, move_rows(): lax.all_to_all(buffer.reshape(experts, rows // experts, cols), ('fsdp', '...  240 us
    reduce_scatter x2, waiting for transfers between devices, scatter_layer(): lax.psum_scatter(both.astype(jnp.bfloat16), ('tensor', 'fsdp'), scatter_d...  219 us
    all_gather x5, waiting for transfers between devices, all_tokens(): return lax.all_gather(array, 'tensor', axis=0, tiled=True)  118 us
    dot_general x26, matrix products, plain_dot(): return jnp.dot(left, right, preferred_element_type=jnp.float32)  102 us
    all_to_all x2, blocking collectives, move_rows(): lax.all_to_all(buffer.reshape(experts, rows // experts, cols), ('fsdp', '...  93.1 us
    dot_general x28, matrix products, contract_first(): lax.dot_general(left, right, (((0,), (0,)), ((), ())), preferred_element_...  72.7 us
    all_gather x2, waiting for transfers between devices, gather_layer(): full = lax.all_gather(packed, ('tensor', 'fsdp'), axis=0, tiled=True)  69.2 us
    reduce_scatter x4, waiting for transfers between devices, sum_own(): return lax.psum_scatter(array, 'tensor', scatter_dimension=0, tiled=True)  64.8 us
  transfers between devices with their start and end apart: 25, of which 19 were waited for; matrix products, arithmetic and copies ran while one was open for 17% of the time, Pallas kernels for 0%

profile of v2, /device:TPU:0, one launch (start us, length us, event | category | flops | bytes accessed | tf_op | source)
XLA Modules:
  0.0 1246.2 jit_solution(16475658155675306257)
XLA Ops:
  11.2 9.7 all-gather
  25.2 69.2 %all-gather.9.cloned.1.call-done = bf16[3072,768]{1,0:T(8,128)(2,1)} async-done(((bf16[192,768]{1,0:T(8,128)(2,1)}), bf16[3072,768]{1,0:T(8,128)(2,1)}) %all-gather.9.cloned.1.call-update) | async-done | bytes 4718608 | tf_op jit(solution)/shard_map/all_gather | solution.py:80
  129.5 28.1 %all-gather.11.cloned.1.call-done = bf16[832,768]{1,0:T(8,128)(2,1)} async-done(((bf16[208,768]{1,0:T(8,128)(2,1)}), bf16[832,768]{1,0:T(8,128)(2,1)}) %all-gather.11.cloned.1.call-update) | async-done | bytes 1277968 | tf_op jit(solution)/shard_map/all_gather | solution.py:160
  170.9 48.2 %all-to-all-done = bf16[8,296,768]{2,1,0:T(8,128)(2,1)} async-done(((bf16[8,296,768]{2,1,0:T(8,128)(2,1)}), bf16[8,296,768]{2,1,0:T(8,128)(2,1)}, u32[]{:S(2)}, u32[]{:S(2)}) %all-to-all-start) | async-done | bytes 3637280 | tf_op jit(solution)/shard_map/all_to_all | solution.py:42
  219.1 21.1 %multiply_convert_fusion.3 = (bf16[2368,768]{1,0:T(8,128)(2,1)S(1)}, f32[2368,768]{1,0:T(8,128)}, f32[2368,768]{1,0:T(8,128)}) fusion(bf16[2368,768]{1,0:T(8,128)(2,1)} %bitcast.50, bf16[2,1,768,768]{3,2,1,0:T(8,128)(2,1)} %param.18), kind=kOutput, calls=%fused_computation.34 | convolution fusion | flops 2911617024 | bytes 23003136 | tf_op jit(solution)/shard_map/dot_general | solution.py:53
  252.6 39.9 %all-to-all-done.1 = bf16[8,296,768]{2,1,0:T(8,128)(2,1)} async-done(((bf16[8,296,768]{2,1,0:T(8,128)(2,1)}), bf16[8,296,768]{2,1,0:T(8,128)(2,1)}, u32[]{:S(2)}, u32[]{:S(2)}) %all-to-all-start.1) | async-done | bytes 3637280 | tf_op jit(solution)/shard_map/all_to_all | solution.py:42
  310.9 19.0 %reduce-scatter.13.cloned.1.call-done = bf16[208,768]{1,0:T(8,128)(2,1)} async-done(((bf16[832,768]{1,0:T(8,128)(2,1)}), bf16[208,768]{1,0:T(8,128)(2,1)}) %reduce-scatter.13.cloned.1.call-update) | async-done | bytes 319504 | tf_op jit(solution)/shard_map/reduce_scatter | solution.py:163
  346.8 31.1 %all-gather.15.cloned.1.call-done = bf16[832,768]{1,0:T(8,128)(2,1)} async-done(((bf16[208,768]{1,0:T(8,128)(2,1)}), bf16[832,768]{1,0:T(8,128)(2,1)}) %all-gather.15.cloned.1.call-update) | async-done | bytes 1277968 | tf_op jit(solution)/shard_map/all_gather | solution.py:160
  384.0 47.2 %all_to_all.40 = bf16[8,296,768]{2,1,0:T(8,128)(2,1)S(1)} all-to-all(bf16[8,296,768]{2,1,0:T(8,128)(2,1)S(1)} %bitcast.700), channel_id=1, replica_groups=mesh['fsdp'=4,'expert'=2,'tensor'=4] {'fsdp','expert'}, dimensions={0} | all-to-all | bytes 7274496 | tf_op jit(solution)/shard_map/all_to_all | solution.py:42
  431.3 19.3 %multiply_convert_fusion.2 = (bf16[2368,768]{1,0:T(8,128)(2,1)S(1)}, f32[2368,768]{1,0:T(8,128)}, f32[2368,768]{1,0:T(8,128)}) fusion(bf16[2368,768]{1,0:T(8,128)(2,1)S(1)} %bitcast.738, bf16[2,1,768,768]{3,2,1,0:T(8,128)(2,1)S(1)} %copy-done.97), kind=kOutput, calls=%fused_computation.21 | convolution fusion | flops 2911617024 | bytes 23003136 | tf_op jit(solution)/shard_map/dot_general | solution.py:53
  463.8 39.1 %all-to-all-done.3 = bf16[8,296,768]{2,1,0:T(8,128)(2,1)} async-done(((bf16[8,296,768]{2,1,0:T(8,128)(2,1)}), bf16[8,296,768]{2,1,0:T(8,128)(2,1)}, u32[]{:S(2)}, u32[]{:S(2)}) %all-to-all-start.3) | async-done | bytes 3637280 | tf_op jit(solution)/shard_map/all_to_all | solution.py:42
  510.1 45.9 %all_to_all.41 = bf16[8,296,768]{2,1,0:T(8,128)(2,1)S(1)} all-to-all(bf16[8,296,768]{2,1,0:T(8,128)(2,1)S(1)} %bitcast.747), channel_id=1, replica_groups=mesh['fsdp'=4,'expert'=2,'tensor'=4] {'fsdp','expert'}, dimensions={0} | all-to-all | bytes 7274496 | tf_op jit(solution)/shard_map/all_to_all | solution.py:42
  556.0 9.3 add_convert_fusion.1
  577.4 40.2 %all-to-all-done.5 = bf16[8,296,768]{2,1,0:T(8,128)(2,1)} async-done(((bf16[8,296,768]{2,1,0:T(8,128)(2,1)}), bf16[8,296,768]{2,1,0:T(8,128)(2,1)}, u32[]{:S(2)}, u32[]{:S(2)}) %all-to-all-start.5) | async-done | bytes 3637280 | tf_op jit(solution)/shard_map/all_to_all | solution.py:42
  638.6 14.3 %reduce-scatter.17.cloned.1.call-done = bf16[208,768]{1,0:T(8,128)(2,1)} async-done(((bf16[832,768]{1,0:T(8,128)(2,1)}), bf16[208,768]{1,0:T(8,128)(2,1)}) %reduce-scatter.17.cloned.1.call-update) | async-done | bytes 319504 | tf_op jit(solution)/shard_map/reduce_scatter | solution.py:163
  655.6 29.7 %reduce-scatter.15.cloned.1.call-done = bf16[208,768]{1,0:T(8,128)(2,1)} async-done(((bf16[832,768]{1,0:T(8,128)(2,1)}), bf16[208,768]{1,0:T(8,128)(2,1)}) %reduce-scatter.15.cloned.1.call-update) | async-done | bytes 319504 | tf_op jit(solution)/shard_map/reduce_scatter | solution.py:163
  710.4 31.1 %all-gather.19.cloned.1.call-done = bf16[832,768]{1,0:T(8,128)(2,1)} async-done(((bf16[208,768]{1,0:T(8,128)(2,1)}), bf16[832,768]{1,0:T(8,128)(2,1)}) %all-gather.19.cloned.1.call-update) | async-done | bytes 1277968 | tf_op jit(solution)/shard_map/all_gather | solution.py:160
  741.5 9.4 fusion.6
  756.1 42.8 %all-to-all-done.6 = bf16[8,296,768]{2,1,0:T(8,128)(2,1)} async-done(((bf16[8,296,768]{2,1,0:T(8,128)(2,1)}), bf16[8,296,768]{2,1,0:T(8,128)(2,1)}, u32[]{:S(2)}, u32[]{:S(2)}) %all-to-all-start.6) | async-done | bytes 3637280 | tf_op jit(solution)/shard_map/all_to_all | solution.py:42
  798.9 11.6 add_convert_fusion
  832.7 30.1 %all-to-all-done.7 = bf16[8,296,768]{2,1,0:T(8,128)(2,1)} async-done(((bf16[8,296,768]{2,1,0:T(8,128)(2,1)}), bf16[8,296,768]{2,1,0:T(8,128)(2,1)}, u32[]{:S(2)}, u32[]{:S(2)}) %all-to-all-start.7) | async-done | bytes 3637280 | tf_op jit(solution)/shard_map/all_to_all | solution.py:42
  976.4 87.9 %reduce-scatter.23.cloned.1.call-done = bf16[112,768]{1,0:T(8,128)(2,1)} async-done(((bf16[1792,768]{1,0:T(8,128)(2,1)}), bf16[112,768]{1,0:T(8,128)(2,1)}) %reduce-scatter.23.cloned.1.call-update) | async-done | bytes 172048 | tf_op jit(solution)/shard_map/reduce_scatter | solution.py:109
  1070.0 27.7 %all-gather.21.cloned.1.call-done = bf16[832,768]{1,0:T(8,128)(2,1)} async-done(((bf16[208,768]{1,0:T(8,128)(2,1)}), bf16[832,768]{1,0:T(8,128)(2,1)}) %all-gather.21.cloned.1.call-update) | async-done | bytes 1277968 | tf_op jit(solution)/shard_map/all_gather | solution.py:160
  1100.9 131.5 %reduce-scatter.21.cloned.1.call-done = bf16[112,768]{1,0:T(8,128)(2,1)} async-done(((bf16[1792,768]{1,0:T(8,128)(2,1)}), bf16[112,768]{1,0:T(8,128)(2,1)}) %reduce-scatter.21.cloned.1.call-update) | async-done | bytes 172048 | tf_op jit(solution)/shard_map/reduce_scatter | solution.py:109
  (533 shorter events, 346.7 us)
Async XLA Ops:
  7.2 87.1 %all-gather.9.cloned.1.call-start = ((), (), s32[]{:S(2)}) async-start(), calls=%async_computation.16 | async-start | bytes 5013504 | tf_op jit(solution)/shard_map/all_gather | solution.py:80
  11.1 146.5 %all-gather.11.cloned.1.call-start = ((), (), s32[]{:S(2)}) async-start(), calls=%async_computation.17 | async-start | bytes 1597440 | tf_op jit(solution)/shard_map/all_gather | solution.py:160
  164.9 54.2 %all-to-all-start = ((bf16[8,296,768]{2,1,0:T(8,128)(2,1)}), bf16[8,296,768]{2,1,0:T(8,128)(2,1)}, u32[]{:S(2)}, u32[]{:S(2)}) async-start(bf16[8,296,768]{2,1,0:T(8,128)(2,1)} %bitcast.699), calls=%async_computation | async-start | bytes 7274496 | tf_op jit(solution)/shard_map/all_to_all | solution.py:42
  169.5 130.8 %all-gather.13.cloned.1.call-start = ((), (), s32[]{:S(2)}) async-start(), calls=%async_computation.19 | async-start | bytes 5013504 | tf_op jit(solution)/shard_map/all_gather | solution.py:80
  244.6 47.8 %all-to-all-start.1 = ((bf16[8,296,768]{2,1,0:T(8,128)(2,1)}), bf16[8,296,768]{2,1,0:T(8,128)(2,1)}, u32[]{:S(2)}, u32[]{:S(2)}) async-start(bf16[8,296,768]{2,1,0:T(8,128)(2,1)} %bitcast.745), calls=%async_computation.1 | async-start | bytes 7274496 | tf_op jit(solution)/shard_map/all_to_all | solution.py:42
  249.3 80.6 %reduce-scatter.13.cloned.1.call-start = ((), (), s32[]{:S(2)}) async-start(), calls=%async_computation.18 | async-start | bytes 1597440 | tf_op jit(solution)/shard_map/reduce_scatter | solution.py:163
  300.0 77.9 %all-gather.15.cloned.1.call-start = ((), (), s32[]{:S(2)}) async-start(), calls=%async_computation.20 | async-start | bytes 1597440 | tf_op jit(solution)/shard_map/all_gather | solution.py:160
  455.0 47.8 %all-to-all-start.3 = ((bf16[8,296,768]{2,1,0:T(8,128)(2,1)}), bf16[8,296,768]{2,1,0:T(8,128)(2,1)}, u32[]{:S(2)}, u32[]{:S(2)}) async-start(bf16[8,296,768]{2,1,0:T(8,128)(2,1)} %bitcast.746), calls=%async_computation.4 | async-start | bytes 7274496 | tf_op jit(solution)/shard_map/all_to_all | solution.py:42
  569.9 47.7 %all-to-all-start.5 = ((bf16[8,296,768]{2,1,0:T(8,128)(2,1)}), bf16[8,296,768]{2,1,0:T(8,128)(2,1)}, u32[]{:S(2)}, u32[]{:S(2)}) async-start(bf16[8,296,768]{2,1,0:T(8,128)(2,1)} %bitcast.744), calls=%async_computation.7 | async-start | bytes 7274496 | tf_op jit(solution)/shard_map/all_to_all | solution.py:42
  574.5 62.1 %reduce-scatter.25.cloned.1.call-start = ((), (), s32[]{:S(2)}) async-start(), calls=%async_computation.29 | async-start | bytes 532480
  577.3 75.5 %reduce-scatter.17.cloned.1.call-start = ((), (), s32[]{:S(2)}) async-start(), calls=%async_computation.23 | async-start | bytes 1597440 | tf_op jit(solution)/shard_map/reduce_scatter | solution.py:163
  624.8 60.6 %reduce-scatter.15.cloned.1.call-start = ((), (), s32[]{:S(2)}) async-start(), calls=%async_computation.21 | async-start | bytes 1597440 | tf_op jit(solution)/shard_map/reduce_scatter | solution.py:163
  632.4 109.1 %all-gather.19.cloned.1.call-start = ((), (), s32[]{:S(2)}) async-start(), calls=%async_computation.24 | async-start | bytes 1597440 | tf_op jit(solution)/shard_map/all_gather | solution.py:160
  750.9 48.0 %all-to-all-start.6 = ((bf16[8,296,768]{2,1,0:T(8,128)(2,1)}), bf16[8,296,768]{2,1,0:T(8,128)(2,1)}, u32[]{:S(2)}, u32[]{:S(2)}) async-start(bf16[8,296,768]{2,1,0:T(8,128)(2,1)} %bitcast.743), calls=%async_computation.9 | async-start | bytes 7274496 | tf_op jit(solution)/shard_map/all_to_all | solution.py:42
  815.0 47.8 %all-to-all-start.7 = ((bf16[8,296,768]{2,1,0:T(8,128)(2,1)}), bf16[8,296,768]{2,1,0:T(8,128)(2,1)}, u32[]{:S(2)}, u32[]{:S(2)}) async-start(bf16[8,296,768]{2,1,0:T(8,128)(2,1)} %bitcast.742), calls=%async_computation.10 | async-start | bytes 7274496 | tf_op jit(solution)/shard_map/all_to_all | solution.py:42
  819.7 69.3 %reduce-scatter.27.cloned.1.call-start = ((), (), s32[]{:S(2)}) async-start(), calls=%async_computation.30 | async-start | bytes 532480
  832.5 65.8 %reduce-scatter.19.cloned.1.call-start = ((), (), s32[]{:S(2)}) async-start(), calls=%async_computation.25 | async-start | bytes 1597440 | tf_op jit(solution)/shard_map/reduce_scatter | solution.py:163
  870.2 86.0 %all-gather.17.cloned.1.call-start = ((), (), s32[]{:S(2)}) async-start(), calls=%async_computation.22 | async-start | bytes 1597440 | tf_op jit(solution)/shard_map/all_gather | solution.py:160
  877.9 14.0 %collective-permute-start.1 = (bf16[1792,768]{1,0:T(8,128)(2,1)}, bf16[1792,768]{1,0:T(8,128)(2,1)}, u32[]{:S(2)}, u32[]{:S(2)}) collective-permute-start(bf16[1792,768]{1,0:T(8,128)(2,1)} %bitcast.235), channel_id=1, source_target_pairs={{0,4},{4,0},{1,5},{5,1},{2,6},{6,2},{3,7},{7,3},{8,12},{12,8},{9,1... | collective-permute-start | bytes 8257544 | tf_op jit(solution)/shard_map/ppermute | solution.py:71
  877.9 186.4 %reduce-scatter.23.cloned.1.call-start = ((), (), s32[]{:S(2)}) async-start(), calls=%async_computation.28 | async-start | bytes 2924544 | tf_op jit(solution)/shard_map/reduce_scatter | solution.py:109
  896.0 201.7 %all-gather.21.cloned.1.call-start = ((), (), s32[]{:S(2)}) async-start(), calls=%async_computation.26 | async-start | bytes 1597440 | tf_op jit(solution)/shard_map/all_gather | solution.py:160
  933.8 5.4 collective-permute-start
  935.9 296.5 %reduce-scatter.21.cloned.1.call-start = ((), (), s32[]{:S(2)}) async-start(), calls=%async_computation.27 | async-start | bytes 2924544 | tf_op jit(solution)/shard_map/reduce_scatter | solution.py:109
  1065.2 4.3 collective-permute-start.3
  (109 other events, 2401.2 us)
Sparse Core Ops, SparseCore 0:
  11.4 82.8 all-gather.8
  126.7 30.7 all-gather.10
  173.7 91.1 all-gather.12
  300.1 29.7 reduce-scatter.12
  347.0 30.8 all-gather.14
  577.5 20.2 reduce-scatter.24
  624.9 27.9 reduce-scatter.16
  655.9 29.4 reduce-scatter.14
  710.5 30.9 all-gather.18
  832.6 20.2 reduce-scatter.26
  870.3 27.9 reduce-scatter.18
  899.7 30.3 all-gather.16
  935.7 128.5 reduce-scatter.22
  1066.4 31.2 all-gather.20
  1103.3 128.9 reduce-scatter.20

commit v3 on v2

--- a/solution.py
+++ b/solution.py
@@ -100,22 +100,40 @@
         tensor_width, fsdp_width, cores, half, cols
     )
     core = lax.axis_index("expert")
-    mine = lax.dynamic_index_in_dim(split, core, 2, keepdims=False)
-    theirs = lax.dynamic_index_in_dim(split, 1 - core, 2, keepdims=False)
     chunk = half + small_rows
-    mine = jnp.concatenate([mine, small], axis=2).reshape(-1, cols)
-    theirs = jnp.concatenate([theirs, small], axis=2).reshape(-1, cols)
-    both = mine.astype(jnp.float32) + swap_cores(theirs).astype(jnp.float32)
+    if cores == 2:
+        mine = lax.dynamic_index_in_dim(split, core, 2, keepdims=False)
+        theirs = lax.dynamic_index_in_dim(split, 1 - core, 2, keepdims=False)
+        mine = jnp.concatenate([mine, small], axis=2).reshape(-1, cols)
+        theirs = jnp.concatenate([theirs, small], axis=2).reshape(-1, cols)
+        both = mine.astype(jnp.float32) + swap_cores(theirs).astype(jnp.float32)
+        both = both.astype(jnp.bfloat16)
+    else:
+        small = jnp.broadcast_to(
+            small[None], (cores, tensor_width, fsdp_width, small_rows, cols)
+        )
+        every = jnp.concatenate([split.transpose(2, 0, 1, 3, 4), small], axis=3)
+        both = lax.psum_scatter(
+            every.reshape(-1, cols), "expert", scatter_dimension=0, tiled=True
+        )
+    both = both.reshape(tensor_width, fsdp_width, chunk, cols)
+    both = lax.all_to_all(both, "fsdp", split_axis=1, concat_axis=1, tiled=True)
+    both = jnp.sum(both.astype(jnp.float32), axis=1).astype(jnp.bfloat16)
     part = lax.psum_scatter(
-        both.astype(jnp.bfloat16), ("tensor", "fsdp"), scatter_dimension=0, tiled=True
+        both.reshape(-1, cols), "tensor", scatter_dimension=0, tiled=True
     )
     small_sum = part[half:chunk].reshape(-1)[: small_count * rows]
     own_half = part[:half]
-    other_half = swap_cores(own_half)
-    upper = core == 1
-    whole = jnp.concatenate(
-        [jnp.where(upper, other_half, own_half), jnp.where(upper, own_half, other_half)], axis=0
-    ).astype(jnp.float32)
+    if cores == 2:
+        other_half = swap_cores(own_half)
+        upper = core == 1
+        whole = jnp.concatenate(
+            [jnp.where(upper, other_half, own_half), jnp.where(upper, own_half, other_half)],
+            axis=0,
+        )
+    else:
+        whole = lax.all_gather(own_half, "expert", axis=0, tiled=True)
+    whole = whole.astype(jnp.float32)
     qkv_cols = cols // 4 * 3
     return (
         whole[:, :qkv_cols].reshape(rows, 3, qkv_cols // 3),

time: 1260 us -> 1050 us (0.83)
  waiting for transfers between devices: 715 us -> 483 us
    reduce_scatter x2, waiting for transfers between devices: 219 us -> 15 us  [scatter_layer(): lax.psum_scatter(both.reshape(-1, cols), 'tensor', scatter_dimension=0, t...]
    all_gather x5, waiting for transfers between devices: 118 us -> 90.2 us  [all_tokens(): return lax.all_gather(array, 'tensor', axis=0, tiled=True)]
  transfers between devices with their start and end apart: 25 -> 27, of which waited for: 19 -> 16; matrix products, arithmetic and copies ran while one was open for 17% -> 22% of each run, Pallas kernels for 0% -> 0%
where the time goes in v3:
time: 1050 us; the launch traced here: 1040 us
  waiting for transfers between devices  483 us (46%)
  matrix products  258 us (25%)
  blocking collectives  103 us (10%)
  local copies, waits for them, and re-layouts  78.5 us (7%)
  other arithmetic  63.1 us (6%)
  starting transfers between devices  39.1 us (4%)
  between operations  16.5 us (2%)
    all_to_all x6, waiting for transfers between devices, move_rows(): lax.all_to_all(buffer.reshape(experts, rows // experts, cols), ('fsdp', '...  239 us
    dot_general x26, matrix products, plain_dot(): return jnp.dot(left, right, preferred_element_type=jnp.float32)  101 us
    all_to_all x2, blocking collectives, move_rows(): lax.all_to_all(buffer.reshape(experts, rows // experts, cols), ('fsdp', '...  93.1 us
    all_gather x5, waiting for transfers between devices, all_tokens(): return lax.all_gather(array, 'tensor', axis=0, tiled=True)  90.2 us
    dot_general x28, matrix products, contract_first(): lax.dot_general(left, right, (((0,), (0,)), ((), ())), preferred_element_...  75.6 us
    all_gather x2, waiting for transfers between devices, gather_layer(): full = lax.all_gather(packed, ('tensor', 'fsdp'), axis=0, tiled=True)  69.4 us
    reduce_scatter x4, waiting for transfers between devices, sum_own(): return lax.psum_scatter(array, 'tensor', scatter_dimension=0, tiled=True)  63.2 us
    dot_general x24, matrix products, contract_last(): lax.dot_general(left, right, (((1,), (1,)), ((), ())), preferred_element_...  62.8 us
  transfers between devices with their start and end apart: 27, of which 16 were waited for; matrix products, arithmetic and copies ran while one was open for 22% of the time, Pallas kernels for 0%

profile of v3, /device:TPU:0, one launch (start us, length us, event | category | flops | bytes accessed | tf_op | source)
XLA Modules:
  0.0 1041.0 jit_solution(16820187770408105667)
XLA Ops:
  11.2 9.7 all-gather
  25.2 69.4 %all-gather.9.cloned.1.call-done = bf16[3072,768]{1,0:T(8,128)(2,1)} async-done(((bf16[192,768]{1,0:T(8,128)(2,1)}), bf16[3072,768]{1,0:T(8,128)(2,1)}) %all-gather.9.cloned.1.call-update) | async-done | bytes 4718608 | tf_op jit(solution)/shard_map/all_gather | solution.py:80
  129.8 28.1 %all-gather.11.cloned.1.call-done = bf16[832,768]{1,0:T(8,128)(2,1)} async-done(((bf16[208,768]{1,0:T(8,128)(2,1)}), bf16[832,768]{1,0:T(8,128)(2,1)}) %all-gather.11.cloned.1.call-update) | async-done | bytes 1277968 | tf_op jit(solution)/shard_map/all_gather | solution.py:178
  171.2 48.2 %all-to-all-done = bf16[8,296,768]{2,1,0:T(8,128)(2,1)} async-done(((bf16[8,296,768]{2,1,0:T(8,128)(2,1)}), bf16[8,296,768]{2,1,0:T(8,128)(2,1)}, u32[]{:S(2)}, u32[]{:S(2)}) %all-to-all-start) | async-done | bytes 3637280 | tf_op jit(solution)/shard_map/all_to_all | solution.py:42
  219.4 21.1 %multiply_convert_fusion.3 = (bf16[2368,768]{1,0:T(8,128)(2,1)S(1)}, f32[2368,768]{1,0:T(8,128)}, f32[2368,768]{1,0:T(8,128)}) fusion(bf16[2368,768]{1,0:T(8,128)(2,1)} %bitcast.50, bf16[2,1,768,768]{3,2,1,0:T(8,128)(2,1)} %param.18), kind=kOutput, calls=%fused_computation.34 | convolution fusion | flops 2911617024 | bytes 23003136 | tf_op jit(solution)/shard_map/dot_general | solution.py:53
  252.8 39.9 %all-to-all-done.1 = bf16[8,296,768]{2,1,0:T(8,128)(2,1)} async-done(((bf16[8,296,768]{2,1,0:T(8,128)(2,1)}), bf16[8,296,768]{2,1,0:T(8,128)(2,1)}, u32[]{:S(2)}, u32[]{:S(2)}) %all-to-all-start.1) | async-done | bytes 3637280 | tf_op jit(solution)/shard_map/all_to_all | solution.py:42
  311.2 18.9 %reduce-scatter.13.cloned.1.call-done = bf16[208,768]{1,0:T(8,128)(2,1)} async-done(((bf16[832,768]{1,0:T(8,128)(2,1)}), bf16[208,768]{1,0:T(8,128)(2,1)}) %reduce-scatter.13.cloned.1.call-update) | async-done | bytes 319504 | tf_op jit(solution)/shard_map/reduce_scatter | solution.py:181
  347.1 31.1 %all-gather.15.cloned.1.call-done = bf16[832,768]{1,0:T(8,128)(2,1)} async-done(((bf16[208,768]{1,0:T(8,128)(2,1)}), bf16[832,768]{1,0:T(8,128)(2,1)}) %all-gather.15.cloned.1.call-update) | async-done | bytes 1277968 | tf_op jit(solution)/shard_map/all_gather | solution.py:178
  384.3 47.2 %all_to_all.50 = bf16[8,296,768]{2,1,0:T(8,128)(2,1)S(1)} all-to-all(bf16[8,296,768]{2,1,0:T(8,128)(2,1)S(1)} %bitcast.704), channel_id=1, replica_groups=mesh['fsdp'=4,'expert'=2,'tensor'=4] {'fsdp','expert'}, dimensions={0} | all-to-all | bytes 7274496 | tf_op jit(solution)/shard_map/all_to_all | solution.py:42
  431.6 19.2 %multiply_convert_fusion.2 = (bf16[2368,768]{1,0:T(8,128)(2,1)S(1)}, f32[2368,768]{1,0:T(8,128)}, f32[2368,768]{1,0:T(8,128)}) fusion(bf16[2368,768]{1,0:T(8,128)(2,1)S(1)} %bitcast.744, bf16[2,1,768,768]{3,2,1,0:T(8,128)(2,1)S(1)} %copy-done.101), kind=kOutput, calls=%fused_computation.21 | convolution fusion | flops 2911617024 | bytes 23003136 | tf_op jit(solution)/shard_map/dot_general | solution.py:53
  464.0 39.1 %all-to-all-done.3 = bf16[8,296,768]{2,1,0:T(8,128)(2,1)} async-done(((bf16[8,296,768]{2,1,0:T(8,128)(2,1)}), bf16[8,296,768]{2,1,0:T(8,128)(2,1)}, u32[]{:S(2)}, u32[]{:S(2)}) %all-to-all-start.3) | async-done | bytes 3637280 | tf_op jit(solution)/shard_map/all_to_all | solution.py:42
  510.4 45.9 %all_to_all.51 = bf16[8,296,768]{2,1,0:T(8,128)(2,1)S(1)} all-to-all(bf16[8,296,768]{2,1,0:T(8,128)(2,1)S(1)} %bitcast.753), channel_id=1, replica_groups=mesh['fsdp'=4,'expert'=2,'tensor'=4] {'fsdp','expert'}, dimensions={0} | all-to-all | bytes 7274496 | tf_op jit(solution)/shard_map/all_to_all | solution.py:42
  556.3 9.3 add_convert_fusion.1
  577.7 40.2 %all-to-all-done.5 = bf16[8,296,768]{2,1,0:T(8,128)(2,1)} async-done(((bf16[8,296,768]{2,1,0:T(8,128)(2,1)}), bf16[8,296,768]{2,1,0:T(8,128)(2,1)}, u32[]{:S(2)}, u32[]{:S(2)}) %all-to-all-start.5) | async-done | bytes 3637280 | tf_op jit(solution)/shard_map/all_to_all | solution.py:42
  638.6 14.5 %reduce-scatter.17.cloned.1.call-done = bf16[208,768]{1,0:T(8,128)(2,1)} async-done(((bf16[832,768]{1,0:T(8,128)(2,1)}), bf16[208,768]{1,0:T(8,128)(2,1)}) %reduce-scatter.17.cloned.1.call-update) | async-done | bytes 319504 | tf_op jit(solution)/shard_map/reduce_scatter | solution.py:181
  656.0 29.7 %reduce-scatter.15.cloned.1.call-done = bf16[208,768]{1,0:T(8,128)(2,1)} async-done(((bf16[832,768]{1,0:T(8,128)(2,1)}), bf16[208,768]{1,0:T(8,128)(2,1)}) %reduce-scatter.15.cloned.1.call-update) | async-done | bytes 319504 | tf_op jit(solution)/shard_map/reduce_scatter | solution.py:181
  711.2 31.1 %all-gather.19.cloned.1.call-done = bf16[832,768]{1,0:T(8,128)(2,1)} async-done(((bf16[208,768]{1,0:T(8,128)(2,1)}), bf16[832,768]{1,0:T(8,128)(2,1)}) %all-gather.19.cloned.1.call-update) | async-done | bytes 1277968 | tf_op jit(solution)/shard_map/all_gather | solution.py:178
  742.3 8.8 fusion.6
  760.9 38.4 %all-to-all-done.6 = bf16[8,296,768]{2,1,0:T(8,128)(2,1)} async-done(((bf16[8,296,768]{2,1,0:T(8,128)(2,1)}), bf16[8,296,768]{2,1,0:T(8,128)(2,1)}, u32[]{:S(2)}, u32[]{:S(2)}) %all-to-all-start.6) | async-done | bytes 3637280 | tf_op jit(solution)/shard_map/all_to_all | solution.py:42
  799.3 11.6 %add_convert_fusion = bf16[2368,768]{1,0:T(8,128)(2,1)S(1)} fusion(f32[2368,768]{1,0:T(8,128)} %get-tuple-element.100, f32[2368,768]{1,0:T(8,128)} %get-tuple-element.149, bf16[2368,768]{1,0:T(8,128)(2,1)} %bitcast.136, bf16[2,1,768,768]{3,2,1,0:T(8,128)(2,1)} %param.19), kind=kOutput, calls=%fused_computation.17 | convolution fusion | flops 2818867200 | bytes 23003136 | tf_op jit(solution)/shard_map/dot_general | solution.py:63
  829.9 33.1 %all-to-all-done.7 = bf16[8,296,768]{2,1,0:T(8,128)(2,1)} async-done(((bf16[8,296,768]{2,1,0:T(8,128)(2,1)}), bf16[8,296,768]{2,1,0:T(8,128)(2,1)}, u32[]{:S(2)}, u32[]{:S(2)}) %all-to-all-start.7) | async-done | bytes 3637280 | tf_op jit(solution)/shard_map/all_to_all | solution.py:42
  976.7 8.1 convolution_bitcast_fusion.3
  992.5 8.3 convolution_bitcast_fusion.1
  1012.2 15.0 %reduce-scatter.21.cloned.1.call-done = bf16[112,768]{1,0:T(8,128)(2,1)} async-done(((bf16[448,768]{1,0:T(8,128)(2,1)}), bf16[112,768]{1,0:T(8,128)(2,1)}) %reduce-scatter.21.cloned.1.call-update) | async-done | bytes 172048 | tf_op jit(solution)/shard_map/reduce_scatter | solution.py:122
  (547 shorter events, 358.6 us)
Async XLA Ops:
  7.2 87.4 %all-gather.9.cloned.1.call-start = ((), (), s32[]{:S(2)}) async-start(), calls=%async_computation.18 | async-start | bytes 5013504 | tf_op jit(solution)/shard_map/all_gather | solution.py:80
  11.1 146.8 %all-gather.11.cloned.1.call-start = ((), (), s32[]{:S(2)}) async-start(), calls=%async_computation.19 | async-start | bytes 1597440 | tf_op jit(solution)/shard_map/all_gather | solution.py:178
  165.2 54.2 %all-to-all-start = ((bf16[8,296,768]{2,1,0:T(8,128)(2,1)}), bf16[8,296,768]{2,1,0:T(8,128)(2,1)}, u32[]{:S(2)}, u32[]{:S(2)}) async-start(bf16[8,296,768]{2,1,0:T(8,128)(2,1)} %bitcast.703), calls=%async_computation | async-start | bytes 7274496 | tf_op jit(solution)/shard_map/all_to_all | solution.py:42
  169.8 130.7 %all-gather.13.cloned.1.call-start = ((), (), s32[]{:S(2)}) async-start(), calls=%async_computation.21 | async-start | bytes 5013504 | tf_op jit(solution)/shard_map/all_gather | solution.py:80
  244.8 47.8 %all-to-all-start.1 = ((bf16[8,296,768]{2,1,0:T(8,128)(2,1)}), bf16[8,296,768]{2,1,0:T(8,128)(2,1)}, u32[]{:S(2)}, u32[]{:S(2)}) async-start(bf16[8,296,768]{2,1,0:T(8,128)(2,1)} %bitcast.751), calls=%async_computation.1 | async-start | bytes 7274496 | tf_op jit(solution)/shard_map/all_to_all | solution.py:42
  249.5 80.6 %reduce-scatter.13.cloned.1.call-start = ((), (), s32[]{:S(2)}) async-start(), calls=%async_computation.20 | async-start | bytes 1597440 | tf_op jit(solution)/shard_map/reduce_scatter | solution.py:181
  300.3 77.9 %all-gather.15.cloned.1.call-start = ((), (), s32[]{:S(2)}) async-start(), calls=%async_computation.22 | async-start | bytes 1597440 | tf_op jit(solution)/shard_map/all_gather | solution.py:178
  455.3 47.8 %all-to-all-start.3 = ((bf16[8,296,768]{2,1,0:T(8,128)(2,1)}), bf16[8,296,768]{2,1,0:T(8,128)(2,1)}, u32[]{:S(2)}, u32[]{:S(2)}) async-start(bf16[8,296,768]{2,1,0:T(8,128)(2,1)} %bitcast.752), calls=%async_computation.4 | async-start | bytes 7274496 | tf_op jit(solution)/shard_map/all_to_all | solution.py:42
  570.2 47.7 %all-to-all-start.5 = ((bf16[8,296,768]{2,1,0:T(8,128)(2,1)}), bf16[8,296,768]{2,1,0:T(8,128)(2,1)}, u32[]{:S(2)}, u32[]{:S(2)}) async-start(bf16[8,296,768]{2,1,0:T(8,128)(2,1)} %bitcast.750), calls=%async_computation.7 | async-start | bytes 7274496 | tf_op jit(solution)/shard_map/all_to_all | solution.py:42
  574.7 61.9 %reduce-scatter.25.cloned.1.call-start = ((), (), s32[]{:S(2)}) async-start(), calls=%async_computation.31 | async-start | bytes 532480
  577.6 75.5 %reduce-scatter.17.cloned.1.call-start = ((), (), s32[]{:S(2)}) async-start(), calls=%async_computation.25 | async-start | bytes 1597440 | tf_op jit(solution)/shard_map/reduce_scatter | solution.py:181
  625.0 60.6 %reduce-scatter.15.cloned.1.call-start = ((), (), s32[]{:S(2)}) async-start(), calls=%async_computation.23 | async-start | bytes 1597440 | tf_op jit(solution)/shard_map/reduce_scatter | solution.py:181
  632.7 109.6 %all-gather.19.cloned.1.call-start = ((), (), s32[]{:S(2)}) async-start(), calls=%async_computation.26 | async-start | bytes 1597440 | tf_op jit(solution)/shard_map/all_gather | solution.py:178
  751.1 48.2 %all-to-all-start.6 = ((bf16[8,296,768]{2,1,0:T(8,128)(2,1)}), bf16[8,296,768]{2,1,0:T(8,128)(2,1)}, u32[]{:S(2)}, u32[]{:S(2)}) async-start(bf16[8,296,768]{2,1,0:T(8,128)(2,1)} %bitcast.748), calls=%async_computation.9 | async-start | bytes 7274496 | tf_op jit(solution)/shard_map/all_to_all | solution.py:42
  815.4 47.7 %all-to-all-start.7 = ((bf16[8,296,768]{2,1,0:T(8,128)(2,1)}), bf16[8,296,768]{2,1,0:T(8,128)(2,1)}, u32[]{:S(2)}, u32[]{:S(2)}) async-start(bf16[8,296,768]{2,1,0:T(8,128)(2,1)} %bitcast.749), calls=%async_computation.10 | async-start | bytes 7274496 | tf_op jit(solution)/shard_map/all_to_all | solution.py:42
  820.0 69.5 %reduce-scatter.27.cloned.1.call-start = ((), (), s32[]{:S(2)}) async-start(), calls=%async_computation.32 | async-start | bytes 532480
  829.9 71.9 %reduce-scatter.19.cloned.1.call-start = ((), (), s32[]{:S(2)}) async-start(), calls=%async_computation.27 | async-start | bytes 1597440 | tf_op jit(solution)/shard_map/reduce_scatter | solution.py:181
  870.3 101.3 %all-gather.17.cloned.1.call-start = ((), (), s32[]{:S(2)}) async-start(), calls=%async_computation.24 | async-start | bytes 1597440 | tf_op jit(solution)/shard_map/all_gather | solution.py:178
  879.5 12.8 %collective-permute-start.1 = (bf16[1792,768]{1,0:T(8,128)(2,1)}, bf16[1792,768]{1,0:T(8,128)(2,1)}, u32[]{:S(2)}, u32[]{:S(2)}) collective-permute-start(bf16[1792,768]{1,0:T(8,128)(2,1)} %bitcast.237), channel_id=1, source_target_pairs={{0,4},{4,0},{1,5},{5,1},{2,6},{6,2},{3,7},{7,3},{8,12},{12,8},{9,1... | collective-permute-start | bytes 8257544 | tf_op jit(solution)/shard_map/ppermute | solution.py:71
  896.6 48.5 %all-to-all-start.9 = ((bf16[4,4,112,768]{3,2,0,1:T(8,128)(2,1)}), bf16[4,4,112,768]{3,2,0,1:T(8,128)(2,1)}, u32[]{:S(2)}, u32[]{:S(2)}) async-start(bf16[4,4,112,768]{3,2,0,1:T(8,128)(2,1)} %copy.340), calls=%async_computation.14 | async-start | bytes 5505024 | tf_op jit(solution)/shard_map/all_to_all | solution.py:120
  901.3 101.9 %reduce-scatter.23.cloned.1.call-start = ((), (), s32[]{:S(2)}) async-start(), calls=%async_computation.30 | async-start | bytes 860160 | tf_op jit(solution)/shard_map/reduce_scatter | solution.py:122
  948.3 60.7 %all-gather.21.cloned.1.call-start = ((), (), s32[]{:S(2)}) async-start(), calls=%async_computation.28 | async-start | bytes 1597440 | tf_op jit(solution)/shard_map/all_gather | solution.py:178
  954.7 36.2 %all-to-all-start.8 = ((bf16[4,4,112,768]{3,2,0,1:T(8,128)(2,1)}), bf16[4,4,112,768]{3,2,0,1:T(8,128)(2,1)S(1)}, u32[]{:S(2)}, u32[]{:S(2)}) async-start(bf16[4,4,112,768]{3,2,0,1:T(8,128)(2,1)} %copy.332), calls=%async_computation.12 | async-start | bytes 5505024 | tf_op jit(solution)/shard_map/all_to_all | solution.py:120
  958.6 68.6 %reduce-scatter.21.cloned.1.call-start = ((), (), s32[]{:S(2)}) async-start(), calls=%async_computation.29 | async-start | bytes 860160 | tf_op jit(solution)/shard_map/reduce_scatter | solution.py:122
  (114 other events, 2251.8 us)
Sparse Core Ops, SparseCore 0:
  11.4 83.1 all-gather.8
  127.0 30.7 all-gather.10
  174.0 91.2 all-gather.12
  300.4 29.7 reduce-scatter.12
  347.2 30.8 all-gather.14
  578.2 20.3 reduce-scatter.24
  625.2 27.9 reduce-scatter.16
  656.2 29.4 reduce-scatter.14
  711.3 30.9 all-gather.18
  830.0 20.3 reduce-scatter.26
  870.4 27.9 reduce-scatter.18
  899.8 30.9 all-gather.16
  948.4 21.7 reduce-scatter.22
  972.3 30.9 all-gather.20
  1005.6 21.5 reduce-scatter.20
